TPU v7x, 128 devices: a whole 4x4x4 slice. The times are simulated.
128 devices in a mesh: dp: 16 (over y_lo, x, core), tensor: 8 (over y_hi, z).
Axes of the slice: x: 4, y: 4 (y_hi: 2, y_lo: 2; y = y_hi * 2 + y_lo), z: 4, core: 2. Of those that a mesh axis runs over, the one named last changes fastest.
Arguments:
- inputs: bfloat16 [512, 8192], P('tensor', 'dp'), may hold values from -6 to 6
- ordering: int32 [512], replicated, may hold values from 0 to 511, each once
- cotangent: float32 [512], P(('dp', 'tensor')), may hold values from -192 to 192
- gate_weight: bfloat16 [8192, 14336], P('dp', 'tensor'), may hold values from -0.0625 to 0.0625
- up_weight: bfloat16 [8192, 14336], P('dp', 'tensor'), may hold values from -0.0625 to 0.0625
- down_weight: bfloat16 [14336, 8192], P('tensor', 'dp'), may hold values from -0.046875 to 0.046875
- value_head: bfloat16 [8192], P('dp'), may hold values from -0.0625 to 0.0625
Outputs:
- scores: float32 [512], P('tensor')
- input_grad: bfloat16 [512, 8192], P(('dp', 'tensor'))
- gate_grad: bfloat16 [8192, 14336], P('dp', 'tensor')
- up_grad: bfloat16 [8192, 14336], P('dp', 'tensor')
- down_grad: bfloat16 [14336, 8192], P('tensor', 'dp')
Inputs may be any that keep to these rules, and one draw needn't show every extreme that they name: `ordering`: each token index appears exactly once.
All inputs are finite; a program needn't handle non-finite values.
Results may differ from a plain program's by a relative error of at most 0.01.
Values may be sent and summed in bfloat16 or wider, within the bound.
A program may use at most 128 MiB of HBM per device.

v0:
```python
import jax
import jax.numpy as jnp
from jax import lax
from jax.sharding import PartitionSpec as P


def activate(gate, up):
    return (gate * jax.nn.sigmoid(gate) * up).astype(jnp.bfloat16)


def unit_grads(gate, up, unit_back):
    sigmoid_part = jax.nn.sigmoid(gate)
    swish = gate * sigmoid_part
    hidden = (swish * up).astype(jnp.bfloat16)
    gate_low = (unit_back * up * sigmoid_part * (1.0 + gate * (1.0 - sigmoid_part))).astype(
        jnp.bfloat16
    )
    up_low = (unit_back * swish).astype(jnp.bfloat16)
    return (hidden, gate_low, up_low)


def contract_rows(left, right):
    return lax.dot_general(
        left, right, (((0,), (0,)), ((), ())), preferred_element_type=jnp.float32
    )


def contract_cols(left, right):
    return lax.dot_general(
        left, right, (((1,), (1,)), ((), ())), preferred_element_type=jnp.float32
    )


def train_layout(values, dp_count, tp_count, each_rows):
    total = values.shape[0]
    return values.reshape(dp_count, tp_count, each_rows).transpose(1, 0, 2).reshape(total)


def per_device(inputs, ordering, cotangent, gate_weight, up_weight, down_weight, value_head):
    dp_count = lax.axis_size("dp")
    tp_count = lax.axis_size("tensor")
    columns = lax.all_gather(inputs, "tensor", axis=0, tiled=True)
    tokens = columns.shape[0]
    each_rows = tokens // (dp_count * tp_count)
    band_rows = tokens // tp_count
    tp_place = lax.axis_index("tensor")
    gate_serve = jnp.dot(columns, gate_weight, preferred_element_type=jnp.float32)
    up_serve = jnp.dot(columns, up_weight, preferred_element_type=jnp.float32)
    gate_share, up_share = (
        lax.psum_scatter(gate_serve, "dp", scatter_dimension=0, tiled=True),
        lax.psum_scatter(up_serve, "dp", scatter_dimension=0, tiled=True),
    )
    hidden_serve = lax.all_gather(activate(gate_share, up_share), "dp", axis=0, tiled=True)
    lifted = lax.psum_scatter(
        jnp.dot(hidden_serve, down_weight, preferred_element_type=jnp.float32).astype(jnp.bfloat16),
        "tensor",
        scatter_dimension=0,
        tiled=True,
    ).astype(jnp.float32)
    head_float = value_head.astype(jnp.float32)
    partial_score = jnp.sum((inputs.astype(jnp.float32) + lifted) * head_float[None, :], axis=1)
    scores = lax.psum(partial_score, "dp")
    train_index = train_layout(ordering, dp_count, tp_count, each_rows)
    chosen = lax.dynamic_slice_in_dim(train_index, tp_place * band_rows, band_rows, 0)
    picked = jnp.take(columns, chosen, axis=0)
    relayed = lax.all_to_all(picked, "dp", split_axis=0, concat_axis=1, tiled=True)
    returned = lax.all_to_all(relayed, "dp", split_axis=1, concat_axis=0, tiled=True)
    train_cols = lax.all_gather(returned, "tensor", axis=0, tiled=True)
    value_all = lax.all_gather(cotangent, ("dp", "tensor"), axis=0, tiled=True)
    value_train = train_layout(value_all, dp_count, tp_count, each_rows)
    out_grad = value_train[:, None] * head_float[None, :]
    out_low = out_grad.astype(jnp.bfloat16)
    unit_back = contract_cols(out_low, down_weight)
    gate_train = jnp.dot(train_cols, gate_weight, preferred_element_type=jnp.float32)
    up_train = jnp.dot(train_cols, up_weight, preferred_element_type=jnp.float32)
    gate_share, up_share, back_share = (
        lax.psum_scatter(gate_train, "dp", scatter_dimension=0, tiled=True),
        lax.psum_scatter(up_train, "dp", scatter_dimension=0, tiled=True),
        lax.psum_scatter(unit_back, "dp", scatter_dimension=0, tiled=True),
    )
    local_parts = unit_grads(gate_share, up_share, back_share)
    hidden_train, gate_low, up_low = (
        lax.all_gather(local_parts[0], "dp", axis=0, tiled=True),
        lax.all_gather(local_parts[1], "dp", axis=0, tiled=True),
        lax.all_gather(local_parts[2], "dp", axis=0, tiled=True),
    )
    down_grad = contract_rows(hidden_train, out_low).astype(jnp.bfloat16)
    gate_grad = contract_rows(train_cols, gate_low).astype(jnp.bfloat16)
    up_grad = contract_rows(train_cols, up_low).astype(jnp.bfloat16)
    summed = lax.psum_scatter(
        contract_cols(gate_low, gate_weight) + contract_cols(up_low, up_weight),
        "tensor",
        scatter_dimension=0,
        tiled=True,
    )
    direct = lax.dynamic_slice_in_dim(out_grad, tp_place * band_rows, band_rows, 0)
    input_rows = (summed + direct).astype(jnp.bfloat16)
    input_grad = lax.all_to_all(input_rows, "dp", split_axis=0, concat_axis=1, tiled=True)
    return (scores, input_grad, gate_grad, up_grad, down_grad)


def solution(mesh):
    placed = (
        P("tensor", "dp"),
        P(),
        P(("dp", "tensor")),
        P("dp", "tensor"),
        P("dp", "tensor"),
        P("tensor", "dp"),
        P("dp"),
    )
    return jax.shard_map(
        per_device,
        mesh=mesh,
        in_specs=placed,
        out_specs=(
            P("tensor"),
            P(("dp", "tensor"), None),
            P("dp", "tensor"),
            P("dp", "tensor"),
            P("tensor", "dp"),
        ),
        check_vma=False,
    )
```

profile of v0, /device:TPU:9, one launch (start us, length us, event | category | flops | bytes accessed | tf_op | source)
XLA Modules:
  0.0 767.3 jit_solution(2764925240045741876)
XLA Ops:
  8.9 66.4 %all-reduce = f32[512]{0:T(512)S(1)} all-reduce(f32[512]{0:T(512)S(1)} %dynamic-update-slice), channel_id=1, replica_groups=mesh['dp'=16,'tensor'=8] {'dp','tensor'}, use_global_device_ids=true, to_apply=%add | all-reduce | flops 512 | bytes 4096
  75.5 4.6 fusion.2
  81.1 29.3 %all_gather.21 = bf16[512,512]{1,0:T(8,128)(2,1)S(1)} all-gather(bf16[64,512]{1,0:T(8,128)(2,1)S(1)} %copy-done.1), channel_id=1, replica_groups=mesh['dp'=16,'tensor'=8] {'tensor'}, dimensions={0}, use_global_device_ids=true | all-gather | bytes 589824 | tf_op jit(solution)/shard_map/all_gather | solution.py:42
  111.4 18.6 %all_to_all.48 = bf16[16,4,512]{2,1,0:T(4,128)(2,1)S(1)} all-to-all(bf16[16,4,512]{2,1,0:T(4,128)(2,1)S(1)} %broadcast_select_fusion), channel_id=1, replica_groups=mesh['dp'=16,'tensor'=8] {'dp'}, dimensions={0} | all-to-all | bytes 131072 | tf_op jit(solution)/shard_map/all_to_all | solution.py:66
  130.0 9.0 %all_to_all.49 = bf16[4,16,512]{2,0,1:T(4,128)(2,1)S(1)} all-to-all(bf16[4,16,512]{2,0,1:T(4,128)(2,1)S(1)} %bitcast.29), channel_id=1, replica_groups=mesh['dp'=16,'tensor'=8] {'dp'}, dimensions={1} | all-to-all | bytes 131072 | tf_op jit(solution)/shard_map/all_to_all | solution.py:67
  139.0 29.8 %all_gather.24 = bf16[512,512]{1,0:T(8,128)(2,1)S(1)} all-gather(bf16[64,512]{1,0:T(8,128)(2,1)S(1)} %all_to_all.40), channel_id=1, replica_groups=mesh['dp'=16,'tensor'=8] {'tensor'}, dimensions={0}, use_global_device_ids=true | all-gather | bytes 589824 | tf_op jit(solution)/shard_map/all_gather | solution.py:68
  168.7 4.5 fusion.7
  173.3 2.9 fusion.8
  176.3 4.4 fusion.6
  180.8 3.0 fusion.5
  183.9 54.3 %reduce-scatter.16.cloned.1.call-done = f32[32,1792]{1,0:T(8,128)} async-done(((f32[512,1792]{1,0:T(8,128)}), f32[32,1792]{1,0:T(8,128)}) %reduce-scatter.16.cloned.1.call-update) | async-done | bytes 229392 | tf_op jit(solution)/shard_map/reduce_scatter | solution.py:78
  238.1 66.8 %reduce-scatter.18.cloned.1.call-done = f32[32,1792]{1,0:T(8,128)} async-done(((f32[512,1792]{1,0:T(8,128)}), f32[32,1792]{1,0:T(8,128)}) %reduce-scatter.18.cloned.1.call-update) | async-done | bytes 229392 | tf_op jit(solution)/shard_map/reduce_scatter | solution.py:77
  304.9 2.0 multiply_convert_fusion
  307.7 63.9 %reduce-scatter.10.cloned.1.call-done = f32[32,1792]{1,0:T(8,128)} async-done(((f32[512,1792]{1,0:T(8,128)}), f32[32,1792]{1,0:T(8,128)}) %reduce-scatter.10.cloned.1.call-update) | async-done | bytes 229392 | tf_op jit(solution)/shard_map/reduce_scatter | solution.py:51
  371.6 66.7 %reduce-scatter.8.cloned.1.call-done = f32[32,1792]{1,0:T(8,128)} async-done(((f32[512,1792]{1,0:T(8,128)}), f32[32,1792]{1,0:T(8,128)}) %reduce-scatter.8.cloned.1.call-update) | async-done | bytes 229392 | tf_op jit(solution)/shard_map/reduce_scatter | solution.py:50
  438.3 1.8 multiply_convert_fusion.3
  440.9 35.3 %all-gather.7.cloned.1.call-done = bf16[512,1792]{1,0:T(8,128)(2,1)} async-done(((bf16[32,1792]{1,0:T(8,128)(2,1)}), bf16[512,1792]{1,0:T(8,128)(2,1)}) %all-gather.7.cloned.1.call-update) | async-done | bytes 1835024 | tf_op jit(solution)/shard_map/all_gather | solution.py:84
  476.2 2.6 fusion.9
  478.9 32.7 %all-gather.9.cloned.1.call-done = bf16[512,1792]{1,0:T(8,128)(2,1)} async-done(((bf16[32,1792]{1,0:T(8,128)(2,1)}), bf16[512,1792]{1,0:T(8,128)(2,1)}) %all-gather.9.cloned.1.call-update) | async-done | bytes 1835024 | tf_op jit(solution)/shard_map/all_gather | solution.py:85
  511.5 4.2 convolution_add_fusion
  516.1 31.3 %all-gather.5.cloned.1.call-done = bf16[512,1792]{1,0:T(8,128)(2,1)} async-done(((bf16[32,1792]{1,0:T(8,128)(2,1)}), bf16[512,1792]{1,0:T(8,128)(2,1)}) %all-gather.5.cloned.1.call-update) | async-done | bytes 1835024 | tf_op jit(solution)/shard_map/all_gather | solution.py:53
  547.4 4.0 convolution_convert_fusion.3
  551.4 31.9 %all-gather.11.cloned.1.call-done = bf16[512,1792]{1,0:T(8,128)(2,1)} async-done(((bf16[32,1792]{1,0:T(8,128)(2,1)}), bf16[512,1792]{1,0:T(8,128)(2,1)}) %all-gather.11.cloned.1.call-update) | async-done | bytes 1835024 | tf_op jit(solution)/shard_map/all_gather | solution.py:83
  583.4 4.1 convolution_convert_fusion
  587.4 2.4 convolution_convert_fusion.2
  589.8 2.4 convolution_convert_fusion.1
  592.2 64.2 %reduce-scatter.20.cloned.1.call-done = f32[64,512]{1,0:T(8,128)} async-done(((f32[512,512]{1,0:T(8,128)}), f32[64,512]{1,0:T(8,128)}) %reduce-scatter.20.cloned.1.call-update) | async-done | bytes 131088 | tf_op jit(solution)/shard_map/reduce_scatter | solution.py:90
  656.4 0.9 add_convert_fusion
  658.0 7.7 all-to-all-start.2
  665.6 64.0 %reduce-scatter.12.cloned.1.call-done = bf16[64,512]{1,0:T(8,128)(2,1)} async-done(((bf16[512,512]{1,0:T(8,128)(2,1)}), bf16[64,512]{1,0:T(8,128)(2,1)}) %reduce-scatter.12.cloned.1.call-update) | async-done | bytes 65552 | tf_op jit(solution)/shard_map/reduce_scatter | solution.py:54
  729.6 1.0 multiply_reduce_fusion
  730.6 29.6 %psum.7 = f32[64]{0:T(128)} all-reduce(f32[64]{0:T(128)S(1)} %multiply_reduce_fusion), channel_id=1, replica_groups=mesh['dp'=16,'tensor'=8] {'dp'}, use_global_device_ids=true, to_apply=%region_4.0 | all-reduce | flops 64 | bytes 512 | tf_op jit(solution)/shard_map/psum | solution.py:62
  (53 shorter events, 7.3 us)
Async XLA Ops:
  7.2 166.2 %copy-start = (bf16[512,1792]{1,0:T(8,128)(2,1)S(1)}, bf16[512,1792]{1,0:T(8,128)(2,1)}, u32[]{:S(2)}) copy-start(bf16[512,1792]{1,0:T(8,128)(2,1)} %param.10) | copy-start | bytes 5505028
  7.2 176.7 %reduce-scatter.14.cloned.1.call-start = ((), (), s32[]{:S(2)}) async-start(), calls=%async_computation.14 | async-start | bytes 3899392 | tf_op jit(solution)/shard_map/reduce_scatter | solution.py:79
  80.1 0.7 copy-start.2
  80.1 1.0 copy-start.1
  80.1 158.0 %reduce-scatter.16.cloned.1.call-start = ((), (), s32[]{:S(2)}) async-start(), calls=%async_computation.15 | async-start | bytes 3899392 | tf_op jit(solution)/shard_map/reduce_scatter | solution.py:78
  173.3 131.7 %reduce-scatter.18.cloned.1.call-start = ((), (), s32[]{:S(2)}) async-start(), calls=%async_computation.16 | async-start | bytes 3899392 | tf_op jit(solution)/shard_map/reduce_scatter | solution.py:77
  176.3 195.4 %reduce-scatter.10.cloned.1.call-start = ((), (), s32[]{:S(2)}) async-start(), calls=%async_computation.11 | async-start | bytes 3899392 | tf_op jit(solution)/shard_map/reduce_scatter | solution.py:51
  180.8 257.5 %reduce-scatter.8.cloned.1.call-start = ((), (), s32[]{:S(2)}) async-start(), calls=%async_computation.10 | async-start | bytes 3899392 | tf_op jit(solution)/shard_map/reduce_scatter | solution.py:50
  183.8 292.4 %all-gather.7.cloned.1.call-start = ((), (), s32[]{:S(2)}) async-start(), calls=%async_computation.17 | async-start | bytes 1949696 | tf_op jit(solution)/shard_map/all_gather | solution.py:84
  306.9 204.6 %all-gather.9.cloned.1.call-start = ((), (), s32[]{:S(2)}) async-start(), calls=%async_computation.18 | async-start | bytes 1949696 | tf_op jit(solution)/shard_map/all_gather | solution.py:85
  307.7 239.8 %all-gather.5.cloned.1.call-start = ((), (), s32[]{:S(2)}) async-start(), calls=%async_computation.12 | async-start | bytes 1949696 | tf_op jit(solution)/shard_map/all_gather | solution.py:53
  440.1 143.3 %all-gather.11.cloned.1.call-start = ((), (), s32[]{:S(2)}) async-start(), calls=%async_computation.20 | async-start | bytes 1949696 | tf_op jit(solution)/shard_map/all_gather | solution.py:83
  440.8 215.6 %reduce-scatter.20.cloned.1.call-start = ((), (), s32[]{:S(2)}) async-start(), calls=%async_computation.19 | async-start | bytes 1179648 | tf_op jit(solution)/shard_map/reduce_scatter | solution.py:90
  515.7 213.9 %reduce-scatter.12.cloned.1.call-start = ((), (), s32[]{:S(2)}) async-start(), calls=%async_computation.13 | async-start | bytes 589824 | tf_op jit(solution)/shard_map/reduce_scatter | solution.py:54
  583.3 4.1 copy-start.3
  587.4 2.4 copy-start.4
  658.0 102.2 %all-to-all-start.2 = ((bf16[16,4,512]{2,1,0:T(4,128)(2,1)}), bf16[16,4,512]{2,1,0:T(4,128)(2,1)S(1)}, u32[]{:S(2)}, u32[]{:S(2)}) async-start(bf16[16,4,512]{2,1,0:T(4,128)(2,1)} %all_to_all.41), calls=%async_computation.9 | async-start | bytes 131072 | tf_op jit(solution)/shard_map/all_to_all | solution.py:98
Sparse Core Ops, SparseCore 0:
  80.2 60.9 reduce-scatter.13
  173.4 64.7 reduce-scatter.15
  240.6 64.3 reduce-scatter.17
  307.2 64.3 reduce-scatter.9
  373.9 64.3 reduce-scatter.7
  440.4 35.7 all-gather.6
  477.9 33.5 all-gather.8
  513.8 33.5 all-gather.4
  549.7 33.5 all-gather.10
  586.8 69.5 reduce-scatter.19
  660.3 69.2 reduce-scatter.11
where the time goes:
time: 770 us; the launch traced here: 767 us
  waiting for transfers between devices  513 us (67%)
  blocking collectives  183 us (24%)
  matrix products  39 us (5%)
  between operations  14 us (2%)
  starting transfers between devices  8.29 us (1%)
    reduce_scatter x1, waiting for transfers between devices, per_device(): lax.psum_scatter(gate_train, 'dp', scatter_dimension=0, tiled=True)  66.8 us
    reduce_scatter x1, waiting for transfers between devices, per_device(): lax.psum_scatter(gate_serve, 'dp', scatter_dimension=0, tiled=True)  66.7 us
    unnamed x1, blocking collectives  66.4 us
    reduce_scatter x1, waiting for transfers between devices, per_device(): lax.psum_scatter(contract_cols(gate_low, gate_weight) + contract_cols(up_...  64.2 us
    reduce_scatter x1, waiting for transfers between devices, per_device(): lax.psum_scatter(jnp.dot(hidden_serve, down_weight, preferred_element_typ...  64 us
    reduce_scatter x1, waiting for transfers between devices, per_device(): lax.psum_scatter(up_serve, 'dp', scatter_dimension=0, tiled=True)  63.9 us
    reduce_scatter x1, waiting for transfers between devices, per_device(): lax.psum_scatter(up_train, 'dp', scatter_dimension=0, tiled=True)  54.3 us
    all_gather x1, waiting for transfers between devices, per_device(): lax.all_gather(local_parts[1], 'dp', axis=0, tiled=True)  35.3 us
  transfers between devices with their start and end apart: 12, of which 10 were waited for; matrix products, arithmetic and copies ran while one was open for 5% of the time, Pallas kernels for 0%

commit v1 on v0

v1 whole, which is shorter than its diff:
```python
import jax
import jax.numpy as jnp
from jax import lax
from jax.sharding import PartitionSpec as P


def per_device(inputs, ordering, cotangent, gate_weight, up_weight, down_weight, value_head):
    dp_count = lax.axis_size("dp")
    tp_count = lax.axis_size("tensor")
    dp_place = lax.axis_index("dp")
    tp_place = lax.axis_index("tensor")
    head = value_head.astype(jnp.float32)
    columns = lax.all_gather(inputs, "tensor", axis=0, tiled=True)
    tokens = columns.shape[0]
    units = gate_weight.shape[1]
    rows = tokens // dp_count
    both_weight = jnp.concatenate([gate_weight, up_weight], axis=1)
    both = jnp.dot(columns, both_weight, preferred_element_type=jnp.float32).astype(jnp.bfloat16)
    both = lax.psum_scatter(both, "dp", scatter_dimension=0, tiled=True).astype(jnp.float32)
    gate, up = both[:, :units], both[:, units:]
    unit_head = lax.psum(jnp.sum(down_weight.astype(jnp.float32) * head[None, :], axis=1), "dp")
    cot_train = lax.all_gather(cotangent, ("dp", "tensor"), axis=0, tiled=True)
    place = (ordering[:, None] == jnp.arange(tokens)[None, :]).astype(jnp.float32)
    cot_serve = jnp.sum(place * cot_train[:, None], axis=0)
    cot = lax.dynamic_slice_in_dim(cot_serve, dp_place * rows, rows, 0)
    sig = jax.nn.sigmoid(gate)
    swish = gate * sig
    hidden = (swish * up).astype(jnp.bfloat16).astype(jnp.float32)
    back = cot[:, None] * unit_head[None, :]
    gate_low = (back * up * sig * (1.0 + gate * (1.0 - sig))).astype(jnp.bfloat16)
    up_low = (back * swish).astype(jnp.bfloat16)
    low = lax.all_gather(jnp.concatenate([gate_low, up_low], axis=1), "dp", axis=0, tiled=True)
    down_vec = lax.psum(jnp.sum(hidden * cot[:, None], axis=0), "dp")
    down_grad = (down_vec[:, None] * head[None, :]).astype(jnp.bfloat16)
    score = jnp.zeros((tokens,), jnp.float32)
    score = lax.dynamic_update_slice_in_dim(
        score, jnp.sum(inputs.astype(jnp.float32) * head[None, :], axis=1), tp_place * inputs.shape[0], 0
    )
    score = score + lax.dynamic_update_slice_in_dim(
        jnp.zeros((tokens,), jnp.float32), jnp.sum(hidden * unit_head[None, :], axis=1), dp_place * rows, 0
    )
    score = lax.psum(score, ("dp", "tensor"))
    scores = lax.dynamic_slice_in_dim(score, tp_place * inputs.shape[0], inputs.shape[0], 0)
    grads = lax.dot_general(
        columns, low, (((0,), (0,)), ((), ())), preferred_element_type=jnp.float32
    ).astype(jnp.bfloat16)
    gate_grad, up_grad = grads[:, :units], grads[:, units:]
    part = lax.dot_general(
        low, both_weight, (((1,), (1,)), ((), ())), preferred_element_type=jnp.float32
    ).astype(jnp.bfloat16)
    each = tokens // (dp_count * tp_count)

    def layout(values):
        return values.reshape(dp_count, tp_count, each).transpose(1, 0, 2).reshape(tokens)

    part = jnp.take(part, layout(ordering), axis=0)
    summed = lax.psum_scatter(part, "tensor", scatter_dimension=0, tiled=True).astype(jnp.float32)
    band = tokens // tp_count
    cot_band = lax.dynamic_slice_in_dim(layout(cot_train), tp_place * band, band, 0)
    input_rows = (summed + cot_band[:, None] * head[None, :]).astype(jnp.bfloat16)
    input_grad = lax.all_to_all(input_rows, "dp", split_axis=0, concat_axis=1, tiled=True)
    return (scores, input_grad, gate_grad, up_grad, down_grad)


def solution(mesh):
    placed = (
        P("tensor", "dp"),
        P(),
        P(("dp", "tensor")),
        P("dp", "tensor"),
        P("dp", "tensor"),
        P("tensor", "dp"),
        P("dp"),
    )
    return jax.shard_map(
        per_device,
        mesh=mesh,
        in_specs=placed,
        out_specs=(
            P("tensor"),
            P(("dp", "tensor"), None),
            P("dp", "tensor"),
            P("dp", "tensor"),
            P("tensor", "dp"),
        ),
        check_vma=False,
    )
```

time: 770 us -> 349 us (0.45)
  waiting for transfers between devices: 513 us -> 59 us
  blocking collectives: 183 us -> 223 us
  matrix products: 39 us -> 13.4 us
  local copies, waits for them, and re-layouts: 4.02 us -> 22.9 us
    reduce_scatter x7 -> x2, waiting for transfers between devices: 380 us -> 56.3 us  [the longest x1 56.3 us: per_device(): lax.psum_scatter(part, 'tensor', scatter_dimension=0, tiled=True)]
    all_gather x4 -> x1, waiting for transfers between devices: 131 us -> 2.62 us  [per_device(): lax.all_gather(jnp.concatenate([gate_low, up_low], axis=1), 'dp', axis=0,...]
    psum x1 -> x3, blocking collectives: 29.6 us -> 121 us  [the longest x1 64 us: per_device(): score = lax.psum(score, ('dp', 'tensor'))]
    all_gather x1 -> x0, blocking collectives: 29.8 us -> none  [per_device(): train_cols = lax.all_gather(returned, 'tensor', axis=0, tiled=True)]
    all_to_all x2 -> x0, blocking collectives: 27.6 us -> none  [the longest x1 18.6 us: per_device(): lax.all_to_all(picked, 'dp', split_axis=0, concat_axis=1, tiled=True)]
    dot_general x11 -> x3, matrix products: 39 us -> 13.4 us  [the longest x1 5.24 us: per_device(): lax.dot_general(low, both_weight, (((1,), (1,)), ((), ())), preferred_ele...]
    unnamed x13 -> x20, local copies, waits for them, and re-layouts: 2.09 us -> 17.1 us
  transfers between devices with their start and end apart: 12 -> 4, of which waited for: 10 -> 2; matrix products, arithmetic and copies ran while one was open for 5% -> 5% of each run, Pallas kernels for 0% -> 0%
where the time goes in v1:
time: 349 us; the launch traced here: 346 us
  blocking collectives  223 us (64%)
  waiting for transfers between devices  59 us (17%)
  local copies, waits for them, and re-layouts  22.9 us (7%)
  between operations  13.9 us (4%)
  matrix products  13.4 us (4%)
  starting transfers between devices  8.05 us (2%)
  other arithmetic  6.28 us (2%)
    unnamed x1, blocking collectives  71.9 us
    psum x1, blocking collectives, per_device(): score = lax.psum(score, ('dp', 'tensor'))  64 us
    reduce_scatter x1, waiting for transfers between devices, per_device(): lax.psum_scatter(part, 'tensor', scatter_dimension=0, tiled=True)  56.3 us
    all_gather x1, blocking collectives, per_device(): columns = lax.all_gather(inputs, 'tensor', axis=0, tiled=True)  29.9 us
    psum x1, blocking collectives, per_device(): down_vec = lax.psum(jnp.sum(hidden * cot[:, None], axis=0), 'dp')  29.3 us
    psum x1, blocking collectives, per_device(): lax.psum(jnp.sum(down_weight.astype(jnp.float32) * head[None, :], axis=1)...  27.6 us
    unnamed x20, local copies, waits for them, and re-layouts  17.1 us
    all_to_all x1, starting transfers between devices, per_device(): lax.all_to_all(input_rows, 'dp', split_axis=0, concat_axis=1, tiled=True)  7.93 us
  transfers between devices with their start and end apart: 4, of which 2 were waited for; matrix products, arithmetic and copies ran while one was open for 5% of the time, Pallas kernels for 0%

profile of v1, /device:TPU:9, one launch (start us, length us, event | category | flops | bytes accessed | tf_op | source)
XLA Modules:
  0.0 346.2 jit_solution(9591175601841539623)
XLA Ops:
  7.2 1.8 constant_dynamic-update-slice_fusion.1
  9.0 29.9 %all_gather.9 = bf16[512,512]{1,0:T(8,128)(2,1)S(1)} all-gather(bf16[64,512]{1,0:T(8,128)(2,1)S(1)} %copy-done.3), channel_id=1, replica_groups=mesh['dp'=16,'tensor'=8] {'tensor'}, dimensions={0}, use_global_device_ids=true | all-gather | bytes 589824 | tf_op jit(solution)/shard_map/all_gather | solution.py:13
  39.1 1.8 copy-done.2
  40.9 4.0 %fusion = bf16[512,3584]{0,1:T(8,128)(2,1)} fusion(bf16[512,3584]{1,0:T(8,128)(2,1)S(1)} %constant_dynamic-update-slice_fusion, bf16[512,512]{1,0:T(8,128)(2,1)S(1)} %all_gather.9), kind=kOutput, calls=%fused_computation.3 | convolution fusion | flops 1880883200 | bytes 7864320 | tf_op jit(solution)/shard_map/dot_general | solution.py:18
  44.9 5.9 %copy.44 = bf16[512,3584]{1,0:T(8,128)(2,1)} copy(bf16[512,3584]{0,1:T(8,128)(2,1)} %fusion) | data formatting | bytes 7340032
  50.9 0.6 copy-done.5
  51.5 0.2 dynamic-update-slice.1
  51.7 71.9 %all-reduce = f32[512]{0:T(512)S(1)} all-reduce(f32[512]{0:T(512)S(1)} %dynamic-update-slice.1), channel_id=1, replica_groups=mesh['dp'=16,'tensor'=8] {'dp','tensor'}, use_global_device_ids=true, to_apply=%add | all-reduce | flops 512 | bytes 4096
  123.6 0.2 select_reduce_fusion
  123.9 0.4 multiply_reduce_fusion
  124.4 27.6 %psum.21 = f32[1792]{0:T(1024)S(1)} all-reduce(f32[1792]{0:T(1024)S(1)} %multiply_reduce_fusion), channel_id=1, replica_groups=mesh['dp'=16,'tensor'=8] {'dp'}, use_global_device_ids=true, to_apply=%region_3.0 | all-reduce | flops 1792 | bytes 14336 | tf_op jit(solution)/shard_map/psum | solution.py:21
  152.0 1.0 convert_element_type.53
  152.9 0.2 fusion.6
  153.1 0.7 pad_maximum_fusion
  154.7 29.3 %psum.23 = f32[1792]{0:T(1024)S(1)} all-reduce(f32[1792]{0:T(1024)S(1)} %get-tuple-element.30), channel_id=1, replica_groups=mesh['dp'=16,'tensor'=8] {'dp'}, use_global_device_ids=true, to_apply=%region_9.10 | all-reduce | flops 1792 | bytes 14336 | tf_op jit(solution)/shard_map/psum | solution.py:33
  184.1 1.5 multiply_convert_fusion
  185.6 2.6 all-gather.2.cloned.1.call-done
  188.2 5.2 %convolution_convert_fusion.2 = bf16[512,512]{1,0:T(8,128)(2,1)S(1)} fusion(bf16[512,3584]{1,0:T(8,128)(2,1)} %all-gather.2.cloned.1.call-done, bf16[512,3584]{1,0:T(8,128)(2,1)} %copy-done.2), kind=kOutput, calls=%fused_computation.7 | convolution fusion | flops 1879310336 | bytes 7864320 | tf_op jit(solution)/shard_map/dot_general | solution.py:48
  193.5 2.0 gather_fusion
  195.4 0.9 broadcast_select_fusion
  196.4 4.1 %fusion.1 = bf16[512,3584]{0,1:T(8,128)(2,1)S(1)} fusion(bf16[512,3584]{1,0:T(8,128)(2,1)} %all-gather.2.cloned.1.call-done, bf16[512,512]{1,0:T(8,128)(2,1)S(1)} %all_gather.9), kind=kOutput, calls=%fused_computation.4 | convolution fusion | flops 1880883200 | bytes 7864320 | tf_op jit(solution)/shard_map/dot_general | solution.py:44
  200.5 1.5 fusion.9
  202.0 3.8 %copy.42 = bf16[512,1792]{1,0:T(8,128)(2,1)} copy(bf16[512,1792]{0,1:T(8,128)(2,1)} %get-tuple-element.33) | data formatting | bytes 3670016
  205.8 2.4 copy.43
  208.2 56.3 %reduce-scatter.5.cloned.1.call-done = bf16[64,512]{1,0:T(8,128)(2,1)} async-done(((bf16[512,512]{1,0:T(8,128)(2,1)}), bf16[64,512]{1,0:T(8,128)(2,1)}) %reduce-scatter.5.cloned.1.call-update) | async-done | bytes 65552 | tf_op jit(solution)/shard_map/reduce_scatter | solution.py:57
  264.5 1.0 add_convert_fusion
  265.5 0.7 all_to_all.14
  266.1 7.9 %all-to-all-start = ((bf16[16,4,512]{2,1,0:T(4,128)(2,1)}), bf16[16,4,512]{2,1,0:T(4,128)(2,1)S(1)}, u32[]{:S(2)}, u32[]{:S(2)}) async-start(bf16[16,4,512]{2,1,0:T(4,128)(2,1)} %all_to_all.14), calls=%async_computation.1 | async-start | bytes 131072 | tf_op jit(solution)/shard_map/all_to_all | solution.py:61
  274.1 0.2 dynamic_update_slice.8
  274.5 64.0 %psum.22 = f32[512]{0:T(512)S(1)} all-reduce(f32[512]{0:T(512)S(1)} %add_dynamic-update-slice_fusion), channel_id=1, replica_groups=mesh['dp'=16,'tensor'=8] {'dp','tensor'}, use_global_device_ids=true, to_apply=%region_5.0 | all-reduce | flops 512 | bytes 4096 | tf_op jit(solution)/shard_map/psum | solution.py:42
  338.5 0.6 dynamic_slice.9
  339.1 0.6 copy.51
  (38 shorter events, 1.4 us)
Async XLA Ops:
  7.2 1.8 copy-start.3
  7.2 31.8 %copy-start = (bf16[512,1792]{1,0:T(8,128)(2,1)S(1)}, bf16[512,1792]{1,0:T(8,128)(2,1)}, u32[]{:S(2)}) copy-start(bf16[512,1792]{1,0:T(8,128)(2,1)} %param.11) | copy-start | bytes 5505028
  7.2 144.8 %reduce-scatter.7.cloned.1.call-start = ((), (), s32[]{:S(2)}) async-start(), calls=%async_computation.5 | async-start | bytes 3899392 | tf_op jit(solution)/shard_map/reduce_scatter | solution.py:19
  39.1 1.8 copy-start.2
  50.8 0.7 copy-start.5
  50.8 0.7 copy-start.6
  50.8 72.8 %copy-start.4 = (s32[512]{0:T(512)S(1)}, s32[512]{0:T(512)}, u32[]{:S(2)}) copy-start(s32[512]{0:T(512)} %param.8) | copy-start | bytes 6148
  50.8 73.1 %copy-start.1 = (bf16[1792,512]{1,0:T(8,128)(2,1)S(1)}, bf16[1792,512]{1,0:T(8,128)(2,1)}, u32[]{:S(2)}) copy-start(bf16[1792,512]{1,0:T(8,128)(2,1)} %param.12) | copy-start | bytes 5505028
  50.9 137.3 %all-gather.2.cloned.1.call-start = ((), (), s32[]{:S(2)}) async-start(), calls=%async_computation.3 | async-start | bytes 3899392 | tf_op jit(solution)/shard_map/all_gather | solution.py:32
  153.8 110.6 %reduce-scatter.5.cloned.1.call-start = ((), (), s32[]{:S(2)}) async-start(), calls=%async_computation.4 | async-start | bytes 589824 | tf_op jit(solution)/shard_map/reduce_scatter | solution.py:57
  266.1 72.9 %all-to-all-start = ((bf16[16,4,512]{2,1,0:T(4,128)(2,1)}), bf16[16,4,512]{2,1,0:T(4,128)(2,1)S(1)}, u32[]{:S(2)}, u32[]{:S(2)}) async-start(bf16[16,4,512]{2,1,0:T(4,128)(2,1)} %all_to_all.14), calls=%async_computation.1 | async-start | bytes 131072 | tf_op jit(solution)/shard_map/all_to_all | solution.py:61
Sparse Core Ops, SparseCore 0:
  51.0 70.0 reduce-scatter.6
  154.0 34.2 all-gather.1
  196.5 67.9 reduce-scatter.4

commit v2 on v1

v2 whole, which is shorter than its diff:
```python
import functools

import jax
import jax.numpy as jnp
from jax import lax
from jax.experimental import pallas as pl
from jax.experimental.pallas import tpu as pltpu
from jax.sharding import PartitionSpec as P

BF = jnp.bfloat16
F32 = jnp.float32
MESH = pl.DeviceIdType.MESH
HALF = 896
CUTS = (0, 640, 1280, 1792)
BLOCKS = 8
ROWS = 64


def slot(part, block):
    bits = [(block >> d) & 1 for d in range(3)]
    return 4 * bits[part] + 2 * bits[(part + 1) % 3] + bits[(part + 2) % 3]


def col_tiles(part):
    lo, hi = CUTS[part], CUTS[part + 1]
    return [(c, min(c + 256, hi)) for c in range(lo, hi, 256)]


def dot(a, b):
    return jnp.dot(a, b, preferred_element_type=F32)


def dot_t(a, b):
    return lax.dot_general(a, b, (((1,), (1,)), ((), ())), preferred_element_type=F32)


def kernel(
    x_in, order_col, order_tile, cot_in, head_in, gate_w, up_w, down_w,
    gate_out, up_out, vec_out, score_out, rows_out,
    xs, xt, wb, down_v, place, rs0, rs1, rs2, rb0, rb1, rb2, lb0, lb1, lb2,
    cot_got, a_send, a_got, sums, b_send, b_got, z_send, z_got, z_perm, t_got, s_send, s_got,
    g_sib, g_own, d_send, d_got,
    x_s, x_r, cot_s, cot_r, xf_s, xf_r, w_s, w_r, loc, rs_s, rs_r, a_s, a_r, ag_s, ag_r, b_s, b_r,
    z_s, z_r, t_s, t_r, sc_s, sc_r, g_s, g_r, d_s, d_r,
):
    rsb, rbb, lbb = (rs0, rs1, rs2), (rb0, rb1, rb2), (lb0, lb1, lb2)
    i = lax.axis_index("dp")
    j = lax.axis_index("tensor")
    core = i % 2
    x = (i // 2) % 4
    y = i // 8
    bits = (((x + 1) // 2) % 2, x // 2, y)
    block = bits[0] + 2 * bits[1] + 4 * bits[2]
    sib = (i + 1 - 2 * core, j)
    near = (
        (y * 8 + (x + 1 - 2 * (x % 2)) * 2 + core, j),
        (y * 8 + (3 - x) * 2 + core, j),
        ((1 - y) * 8 + x * 2 + core, j),
    )

    def xor(v, k, width):
        out = 0
        for b in range(width):
            bit = (v // (1 << b)) % 2
            out = out + ((1 - bit) if (k >> b) & 1 else bit) * (1 << b)
        return out

    t_peer = [None] + [(i, xor(j, k, 3)) for k in range(1, 8)]
    d_peer = [None] + [(xor(i, k, 4), j) for k in range(1, 16)]

    def remote(src, dst, send, recv, device):
        return pltpu.make_async_remote_copy(
            src_ref=src, dst_ref=dst, send_sem=send, recv_sem=recv, device_id=device, device_id_type=MESH
        )

    mine = pl.ds(pl.multiple_of(core * HALF, 128), HALF)
    other = pl.ds(pl.multiple_of((1 - core) * HALF, 128), HALF)

    barrier = pltpu.get_barrier_semaphore()
    for device in t_peer[1:] + d_peer[1:]:
        pl.semaphore_signal(barrier, inc=1, device_id=device, device_id_type=MESH)
    local = [
        pltpu.make_async_copy(down_w, down_v, loc.at[0]),
        pltpu.make_async_copy(gate_w.at[:, mine], wb.at[0, :, pl.ds(0, HALF)], loc.at[1]),
        pltpu.make_async_copy(up_w.at[:, mine], wb.at[0, :, pl.ds(HALF, HALF)], loc.at[2]),
    ]
    for copy in local:
        copy.start()
    head_rows = jnp.broadcast_to(head_in[...], (16, 512))
    x_head = dot_t(head_rows, x_in[...])
    xs[0, pl.ds(j, 1)] = x_in[...][None]
    local[0].wait()
    a_send[...] = jnp.zeros_like(a_send)
    a_send[0, 0:1, :] = dot_t(head_rows, down_v[mine, :])[0:1]
    a_send[1, 0:1, :] = dot_t(head_rows, down_v[other, :])[0:1]
    for v in range(2):
        a_send[v, 1:2, 0:ROWS] = x_head[0:1]
    place[...] = (order_col[...] == lax.broadcasted_iota(jnp.int32, (512, 512), 1)).astype(BF)
    pl.semaphore_wait(barrier, 22)

    x_copies = [None]
    cot_copies = [None]
    for k in range(1, 8):
        x_copies.append(remote(x_in, xs.at[0, j], x_s.at[k - 1], x_r.at[k - 1], t_peer[k]))
        x_copies[k].start()
    for k in range(1, 8):
        cot_copies.append(remote(cot_in, cot_got.at[k - 1], cot_s.at[k - 1], cot_r.at[k - 1], t_peer[k]))
        cot_copies[k].start()
    w_copies = [
        remote(gate_w.at[:, other], wb.at[1, :, pl.ds(0, HALF)], w_s.at[0], w_r.at[0], sib),
        remote(up_w.at[:, other], wb.at[1, :, pl.ds(HALF, HALF)], w_s.at[1], w_r.at[1], sib),
    ]
    forward = [remote(x_in, xs.at[1, j], xf_s.at[0], xf_r.at[0], sib)]
    forward[0].start()
    for copy in w_copies:
        copy.start()
    for k in range(1, 8):
        x_copies[k].wait_recv()
        there = xor(j, k, 3)
        forward.append(remote(xs.at[0, there], xs.at[1, there], xf_s.at[k], xf_r.at[k], sib))
        forward[k].start()
    for k in range(1, 8):
        cot_copies[k].wait_recv()
    cot_part = cot_in[...]
    for k in range(7):
        cot_part = cot_part + cot_got[k]
    for v in range(2):
        a_send[v, 4:8, 0:128] = cot_part[0:4]
    a_copies = [remote(a_send.at[1], a_got.at[0], a_s.at[0], a_r.at[0], sib)]
    a_copies[0].start()
    for copy in local[1:]:
        copy.wait()
    for copy in w_copies:
        copy.wait_recv()
    for copy in forward:
        copy.wait_recv()

    rs_copies = {}

    def rs_start(p, s):
        b0, b1, b2 = bits[p], bits[(p + 1) % 3], bits[(p + 2) % 3]
        first, count, land = (
            (4 * (1 - b0), 4, 0), (4 * b0 + 2 * (1 - b1), 2, 4), (4 * b0 + 2 * b1 + 1 - b2, 1, 6),
        )[s]
        rs_copies[p, s] = remote(
            rsb[p].at[pl.ds(first, count)], rbb[p].at[pl.ds(land, count)],
            rs_s.at[3 * p + s], rs_r.at[3 * p + s], near[(p + s) % 3],
        )
        rs_copies[p, s].start()

    x_own = xs[0].reshape(512, 512)
    x_sib = xs[1].reshape(512, 512)
    for p in range(3):
        for lo, hi in col_tiles(p):
            part = (dot(x_own, wb[0, :, lo:hi]) + dot(x_sib, wb[1, :, lo:hi])).astype(BF)
            for blk in range(BLOCKS):
                rsb[p][slot(p, blk), :, lo - CUTS[p]:hi - CUTS[p]] = part[blk * ROWS:(blk + 1) * ROWS]
        rs_start(p, 0)

    a_copies[0].wait()
    a_send[2] = a_send[0] + a_got[0]
    a_copies.append(remote(a_send.at[2], a_got.at[1], a_s.at[1], a_r.at[1], near[0]))
    a_copies[1].start()

    for v in range(2):
        for c in range(0, 512, 128):
            xt[v, c:c + 128, :] = xs[v, :, :, c:c + 128].reshape(512, 128).T

    for s in range(2):
        for p in range(3):
            b0, b1, b2 = bits[p], bits[(p + 1) % 3], bits[(p + 2) % 3]
            rs_copies[p, s].wait_recv()
            base = 4 * b0 if s == 0 else 4 * b0 + 2 * b1
            land = 0 if s == 0 else 4
            half = 2 if s == 0 else 1
            turn = b1 if s == 0 else b2
            out = pl.ds(base + half * (1 - turn), half)
            got = pl.ds(land + half * (1 - turn), half)
            rsb[p][out] = (rsb[p][out].astype(F32) + rbb[p][got].astype(F32)).astype(BF)
            rs_start(p, s + 1)
        a_copies[s + 1].wait_recv()
        a_send[s + 3] = a_send[s + 2] + a_got[s + 1]
        a_copies.append(remote(a_send.at[s + 3], a_got.at[s + 2], a_s.at[s + 2], a_r.at[s + 2], near[s + 1]))
        a_copies[s + 2].start()
        for p in range(3):
            b0, b1, b2 = bits[p], bits[(p + 1) % 3], bits[(p + 2) % 3]
            base = 4 * b0 if s == 0 else 4 * b0 + 2 * b1
            land = 0 if s == 0 else 4
            half = 2 if s == 0 else 1
            turn = b1 if s == 0 else b2
            keep = pl.ds(base + half * turn, half)
            got = pl.ds(land + half * turn, half)
            rsb[p][keep] = (rsb[p][keep].astype(F32) + rbb[p][got].astype(F32)).astype(BF)
    a_copies[3].wait_recv()
    a_sum = a_send[4] + a_got[3]
    unit_head = a_sum[0:1, :]
    cots = a_sum[4:8, 0:128]
    lanes = lax.broadcasted_iota(jnp.int32, (ROWS, 128), 1)
    subs = lax.broadcasted_iota(jnp.int32, (ROWS, 128), 0)
    serve = jnp.zeros((ROWS, 128), F32)
    train = jnp.zeros((ROWS, 128), F32)
    train_k = 32 * (subs // 4) + 4 * j + subs % 4
    for r in range(4):
        row = jnp.broadcast_to(cots[r:r + 1], (ROWS, 128))
        serve = serve + jnp.where(order_tile[r:r + 1, :] == subs + block * ROWS, row, 0.0)
        train = train + jnp.where(lanes + 128 * r == train_k, row, 0.0)
    cot_serve = jnp.sum(serve, axis=1, keepdims=True)
    cot_train = jnp.sum(train, axis=1, keepdims=True)

    for p in range(3):
        b0, b1, b2 = bits[p], bits[(p + 1) % 3], bits[(p + 2) % 3]
        rs_copies[p, 2].wait_recv()
        here = pl.ds(4 * b0 + 2 * b1 + b2, 1)
        sums[:, CUTS[p]:CUTS[p + 1]] = (rsb[p][here].astype(F32) + rbb[p][6:7].astype(F32))[0]

    gate, up = sums[:, 0:HALF], sums[:, HALF:2 * HALF]
    sig = jax.nn.sigmoid(gate)
    swish = gate * sig
    hidden = (swish * up).astype(BF).astype(F32)
    back = cot_serve * unit_head
    gate_low = (back * up * sig * (1.0 + gate * (1.0 - sig))).astype(BF)
    up_low = (back * swish).astype(BF)
    low = jnp.concatenate([gate_low, up_low], axis=1)

    ag_copies = {}

    def ag_start(p, s):
        b0, b1, b2 = bits[p], bits[(p + 1) % 3], bits[(p + 2) % 3]
        first, count = ((4 * b0 + 2 * b1 + b2, 1), (4 * b0 + 2 * b1, 2), (4 * b0, 4))[s]
        where = lbb[p].at[pl.ds(first, count)]
        ag_copies[p, s] = remote(where, where, ag_s.at[3 * p + s], ag_r.at[3 * p + s], near[(p + 2 - s) % 3])
        ag_copies[p, s].start()

    for p in range(3):
        b0, b1, b2 = bits[p], bits[(p + 1) % 3], bits[(p + 2) % 3]
        lbb[p][pl.ds(4 * b0 + 2 * b1 + b2, 1)] = low[:, CUTS[p]:CUTS[p + 1]][None]
        ag_start(p, 0)

    b_send[...] = jnp.zeros_like(b_send)
    b_send[0, 0:1, :] = jnp.sum(hidden * cot_serve, axis=0, keepdims=True)
    score_col = jnp.sum(hidden * unit_head, axis=1, keepdims=True)
    score_row = jnp.sum(jnp.where(lanes == subs, score_col, 0.0), axis=0, keepdims=True)
    subs8 = lax.broadcasted_iota(jnp.int32, (8, 128), 0)
    b_send[0, 8:16, 0:128] = jnp.where(subs8 == block, score_row, 0.0)
    b_copies = [remote(b_send.at[0], b_got.at[0], b_s.at[0], b_r.at[0], near[0])]
    b_copies[0].start()

    for s in range(2):
        for p in range(3):
            ag_copies[p, s].wait_recv()
            ag_start(p, s + 1)
        b_copies[s].wait_recv()
        b_send[s + 1] = b_send[s] + b_got[s]
        b_copies.append(remote(b_send.at[s + 1], b_got.at[s + 1], b_s.at[s + 1], b_r.at[s + 1], near[s + 1]))
        b_copies[s + 1].start()
    b_copies[2].wait_recv()
    b_send[3] = b_send[2] + b_got[2]
    b_copies.append(remote(b_send.at[3], b_got.at[3], b_s.at[3], b_r.at[3], sib))
    b_copies[3].start()
    for p in range(3):
        ag_copies[p, 2].wait_recv()

    lows = [jnp.concatenate([lbb[p][slot(p, blk)] for blk in range(BLOCKS)], axis=0) for p in range(3)]

    def back_tile(v, lo):
        total = dot_t(lows[0], wb[v, lo:lo + 256, CUTS[0]:CUTS[1]])
        for p in (1, 2):
            total = total + dot_t(lows[p], wb[v, lo:lo + 256, CUTS[p]:CUTS[p + 1]])
        return total

    z_copies = []
    for n, lo in enumerate((0, 256)):
        z_send[n] = back_tile(1, lo).astype(BF)
        z_copies.append(remote(z_send.at[n], z_got.at[n], z_s.at[n], z_r.at[n], sib))
        z_copies[n].start()
    for n, lo in enumerate((0, 256)):
        total = back_tile(0, lo)
        z_copies[n].wait_recv()
        z_perm[:, lo:lo + 256] = dot(place[...], (total + z_got[n].astype(F32)).astype(BF)).astype(BF)
    t_copies = [None]
    for k in range(1, 8):
        there = xor(j, k, 3)
        rows = pl.ds(pl.multiple_of(there * ROWS, ROWS), ROWS)
        t_copies.append(remote(z_perm.at[rows], t_got.at[k - 1], t_s.at[k - 1], t_r.at[k - 1], t_peer[k]))
        t_copies[k].start()
    b_copies[3].wait_recv()
    vec_out[pl.ds(core, 1)] = b_send[3, 0:8, :][None]
    vec_out[pl.ds(1 - core, 1)] = b_got[3, 0:8, :][None]
    s_send[...] = b_send[3, 8:16, 0:128] + b_got[3, 8:16, 0:128]
    sc_copies = [None]
    for k in range(1, 8):
        sc_copies.append(remote(s_send, s_got.at[k - 1], sc_s.at[k - 1], sc_r.at[k - 1], t_peer[k]))
        sc_copies[k].start()

    for p in range(3):
        for lo, hi in col_tiles(p):
            g_sib[:, lo:hi] = dot(xt[1], lows[p][:, lo - CUTS[p]:hi - CUTS[p]]).astype(BF)
    g_copies = [
        remote(g_sib.at[:, pl.ds(0, HALF)], gate_out.at[:, mine], g_s.at[0], g_r.at[0], sib),
        remote(g_sib.at[:, pl.ds(HALF, HALF)], up_out.at[:, mine], g_s.at[1], g_r.at[1], sib),
    ]
    for copy in g_copies:
        copy.start()
    for p in range(3):
        for lo, hi in col_tiles(p):
            g_own[:, lo:hi] = dot(xt[0], lows[p][:, lo - CUTS[p]:hi - CUTS[p]]).astype(BF)
    g_local = [
        pltpu.make_async_copy(g_own.at[:, pl.ds(0, HALF)], gate_out.at[:, mine], loc.at[3]),
        pltpu.make_async_copy(g_own.at[:, pl.ds(HALF, HALF)], up_out.at[:, mine], loc.at[4]),
    ]
    for copy in g_local:
        copy.start()

    total = z_perm[pl.ds(pl.multiple_of(j * ROWS, ROWS), ROWS)].astype(F32)
    for k in range(1, 8):
        t_copies[k].wait_recv()
        total = total + t_got[k - 1].astype(F32)
    total = total + cot_train * head_in[...].astype(F32)
    low_rows = total.astype(BF)
    stacked = jnp.concatenate([low_rows[:, c:c + 128] for c in range(0, 512, 128)], axis=0)
    want = lax.broadcasted_iota(jnp.int32, (256, 256), 0)
    have = lax.broadcasted_iota(jnp.int32, (256, 256), 1)
    source = ((want // 4) % 4) * 64 + (want // 16) * 4 + want % 4
    d_send[...] = dot((have == source).astype(BF), stacked).astype(BF).reshape(16, 16, 128)
    d_copies = [None]
    for k in range(1, 16):
        there = xor(i, k, 4)
        d_copies.append(remote(d_send.at[there], d_got.at[i], d_s.at[k - 1], d_r.at[k - 1], d_peer[k]))
        d_copies[k].start()
    d_got[pl.ds(i, 1)] = d_send[pl.ds(i, 1)]

    score = s_send[...]
    for k in range(1, 8):
        sc_copies[k].wait_recv()
        score = score + s_got[k - 1]
    score = jnp.sum(jnp.where(subs8 == j, score, 0.0), axis=0, keepdims=True)
    score_out[...] = jnp.broadcast_to(score + a_sum[1:2, 0:128], (8, 128))

    for k in range(1, 16):
        d_copies[k].wait_recv()
    rows_out[...] = d_got[...]

    sent = x_copies[1:] + cot_copies[1:] + w_copies + forward + a_copies[1:] + b_copies + z_copies
    sent = sent + t_copies[1:] + sc_copies[1:] + d_copies[1:]
    sent = sent + [rs_copies[p, s] for p in range(3) for s in range(3)]
    sent = sent + [ag_copies[p, s] for p in range(3) for s in range(3)]
    for copy in sent:
        copy.wait_send()
    for copy in g_copies:
        copy.wait()
    for copy in g_local:
        copy.wait()


def per_device(inputs, ordering, cotangent, gate_weight, up_weight, down_weight, value_head):
    i = lax.axis_index("dp")
    j = lax.axis_index("tensor")
    order_col = ordering.reshape(16, 8, 4).transpose(1, 0, 2).reshape(512, 1)
    order_tile = jnp.pad(ordering.reshape(4, 128), ((0, 4), (0, 0)))
    spot = jnp.arange(512, dtype=jnp.int32) - (32 * i + 4 * j)
    cot = sum(jnp.where(spot == r, cotangent[r], 0.0) for r in range(4))
    cot_tile = jnp.pad(cot.reshape(4, 128), ((0, 4), (0, 0)))
    whole = pl.BlockSpec(memory_space=pl.ANY)
    held = pl.BlockSpec(memory_space=pltpu.VMEM)
    dma = pltpu.SemaphoreType.DMA
    widths = [CUTS[p + 1] - CUTS[p] for p in range(3)]
    gate_grad, up_grad, vec, score, rows = pl.pallas_call(
        kernel,
        name="critic",
        out_shape=(
            jax.ShapeDtypeStruct((512, 1792), BF),
            jax.ShapeDtypeStruct((512, 1792), BF),
            jax.ShapeDtypeStruct((2, 8, HALF), F32),
            jax.ShapeDtypeStruct((8, 128), F32),
            jax.ShapeDtypeStruct((16, 16, 128), BF),
        ),
        in_specs=[held] * 5 + [whole] * 3,
        out_specs=(whole, whole, held, held, held),
        scratch_shapes=[
            pltpu.VMEM((2, 8, ROWS, 512), BF),
            pltpu.VMEM((2, 512, 512), BF),
            pltpu.VMEM((2, 512, 2 * HALF), BF),
            pltpu.VMEM((2 * HALF, 512), BF),
            pltpu.VMEM((512, 512), BF),
            *[pltpu.VMEM((8, ROWS, w), BF) for w in widths],
            *[pltpu.VMEM((7, ROWS, w), BF) for w in widths],
            *[pltpu.VMEM((8, ROWS, w), BF) for w in widths],
            pltpu.VMEM((7, 8, 128), F32),
            pltpu.VMEM((5, 8, HALF), F32),
            pltpu.VMEM((4, 8, HALF), F32),
            pltpu.VMEM((ROWS, 2 * HALF), F32),
            pltpu.VMEM((4, 16, HALF), F32),
            pltpu.VMEM((4, 16, HALF), F32),
            pltpu.VMEM((2, 512, 256), BF),
            pltpu.VMEM((2, 512, 256), BF),
            pltpu.VMEM((512, 512), BF),
            pltpu.VMEM((7, ROWS, 512), BF),
            pltpu.VMEM((8, 128), F32),
            pltpu.VMEM((7, 8, 128), F32),
            pltpu.VMEM((512, 2 * HALF), BF),
            pltpu.VMEM((512, 2 * HALF), BF),
            pltpu.VMEM((16, 16, 128), BF),
            pltpu.VMEM((16, 16, 128), BF),
            dma((7,)), dma((7,)), dma((7,)), dma((7,)), dma((8,)), dma((8,)), dma((2,)), dma((2,)),
            dma((5,)), dma((9,)), dma((9,)), dma((4,)), dma((4,)), dma((9,)), dma((9,)), dma((4,)), dma((4,)),
            dma((2,)), dma((2,)), dma((7,)), dma((7,)), dma((7,)), dma((7,)), dma((2,)), dma((2,)),
            dma((15,)), dma((15,)),
        ],
        compiler_params=pltpu.CompilerParams(
            collective_id=0, has_side_effects=True, vmem_limit_bytes=56 * 2**20
        ),
        cost_estimate=pl.CostEstimate(flops=6 * 10**9, bytes_accessed=12 * 10**6, transcendentals=10**5),
    )(inputs, order_col, order_tile, cot_tile, value_head.reshape(1, 512), gate_weight, up_weight, down_weight)
    down_grad = (vec[:, 0, :].reshape(2 * HALF)[:, None] * value_head.astype(F32)[None, :]).astype(BF)
    input_grad = rows.reshape(16, 4, 4, 128).transpose(2, 0, 1, 3).reshape(4, 8192)
    return (score[0, :ROWS], input_grad, gate_grad, up_grad, down_grad)


def solution(mesh):
    placed = (
        P("tensor", "dp"),
        P(),
        P(("dp", "tensor")),
        P("dp", "tensor"),
        P("dp", "tensor"),
        P("tensor", "dp"),
        P("dp"),
    )
    return jax.shard_map(
        per_device,
        mesh=mesh,
        in_specs=placed,
        out_specs=(
            P("tensor"),
            P(("dp", "tensor"), None),
            P("dp", "tensor"),
            P("dp", "tensor"),
            P("tensor", "dp"),
        ),
        check_vma=False,
    )
```

time: 349 us -> 96.6 us (0.28)
  blocking collectives: 223 us -> 0 us
  Pallas kernels: 0 us -> 76.8 us
  waiting for transfers between devices: 59 us -> 0 us
  matrix products: 13.4 us -> 0 us
  between operations: 13.9 us -> 0.68 us
  local copies, waits for them, and re-layouts: 22.9 us -> 13.3 us
  starting transfers between devices: 8.05 us -> 0 us
    psum x3 -> x0, blocking collectives: 121 us -> none  [the longest x1 64 us: per_device(): score = lax.psum(score, ('dp', 'tensor'))]
    pallas_call x0 -> x1, Pallas kernels: none -> 76.8 us  [per_device(): pl.pallas_call(kernel, name='critic', out_shape=(jax.ShapeDtypeStruct((51...]
    unnamed x1 -> x0, blocking collectives: 71.9 us -> none
    reduce_scatter x2 -> x0, waiting for transfers between devices: 56.3 us -> none  [the longest x1 56.3 us: per_device(): lax.psum_scatter(part, 'tensor', scatter_dimension=0, tiled=True)]
    all_gather x1 -> x0, blocking collectives: 29.9 us -> none  [per_device(): columns = lax.all_gather(inputs, 'tensor', axis=0, tiled=True)]
    dot_general x3 -> x0, matrix products: 13.4 us -> none  [the longest x1 5.24 us: per_device(): lax.dot_general(low, both_weight, (((1,), (1,)), ((), ())), preferred_ele...]
    unnamed x20 -> x9, local copies, waits for them, and re-layouts: 17.1 us -> 4.89 us
    all_to_all x1 -> x0, starting transfers between devices: 7.93 us -> none  [per_device(): lax.all_to_all(input_rows, 'dp', split_axis=0, concat_axis=1, tiled=True)]
  transfers between devices with their start and end apart: 4 -> 0, of which waited for: 2 -> 0; matrix products, arithmetic and copies ran while one was open for 5% -> 0% of each run, Pallas kernels for 0% -> 0%
where the time goes in v2:
time: 96.6 us; the launch traced here: 94.9 us
  Pallas kernels  76.8 us (80%)
  local copies, waits for them, and re-layouts  13.3 us (14%)
  other arithmetic  4.12 us (4%)
    pallas_call x1, Pallas kernels, per_device(): pl.pallas_call(kernel, name='critic', out_shape=(jax.ShapeDtypeStruct((51...  76.8 us
    unnamed x9, local copies, waits for them, and re-layouts  4.89 us
    add x1, other arithmetic, per_device(): cot = sum((jnp.where(spot == r, cotangent[r], 0.0) for r in range(4)))  2.58 us

profile of v2, /device:TPU:9, one launch (start us, length us, event | category | flops | bytes accessed | tf_op | source)
XLA Modules:
  0.0 94.9 jit_solution(4211931708026579600)
XLA Ops:
  0.6 0.8 reshape.32
  1.4 0.8 reshape.38.order_col
  2.3 1.3 %pad.8.order_tile = s32[8,128]{1,0:T(8,128)} pad(s32[4,128]{1,0:T(4,128)} %bitcast.15, s32[]{:T(128)} %constant.5.clone.1), padding=0_4x0_0 | pad | bytes 6148 | tf_op jit(solution)/shard_map/jit(_pad)/pad | solution.py:359
  3.5 1.5 %fusion.4 = (f32[1]{0:T(128)}, f32[1]{0:T(128)}, f32[1]{0:T(128)}, f32[1]{0:T(128)}) fusion(f32[4]{0:T(128)} %param.9), kind=kLoop, calls=%fused_computation.9 | loop fusion | bytes 32 | tf_op jit(solution)/shard_map/slice | solution.py:361
  5.0 2.6 %select_add_fusion = f32[4,128]{1,0:T(4,128)S(1)} fusion(f32[]{:T(128)} %bitcast.5, f32[]{:T(128)} %bitcast.4, f32[]{:T(128)} %bitcast.3, f32[]{:T(128)} %bitcast.2, s32[]{:T(128)S(6)} %add.20), kind=kLoop, calls=%fused_computation.2 | loop fusion | flops 7168 | bytes 2068 | tf_op jit(solution)/shard_map/add | solution.py:361
  7.6 0.6 pad.9.cot_in
  8.2 1.3 %reshape.35.head_in = bf16[1,512]{1,0:T(2,128)(2,1)} reshape(bf16[512]{0:T(512)(128)(2,1)} %param.13) | data formatting | bytes 2048 | tf_op jit(solution)/shard_map/reshape | solution.py:413
  9.4 0.0 copy-start.2
  9.4 76.8 %critic.1 = (bf16[512,1792]{1,0:T(8,128)(2,1)}, bf16[512,1792]{1,0:T(8,128)(2,1)}, f32[2,8,896]{2,1,0:T(8,128)}, f32[8,128]{1,0:T(8,128)}, bf16[16,16,128]{2,1,0:T(8,128)(2,1)}) custom-call(bf16[64,512]{1,0:T(8,128)(2,1)} %x_in.1, s32[512,1]{1,0:T(8,128)} %reshape.38.order_col, s32[8,128]{1,0:T(8,128)} %pad.8.order_tile, f32[8,128]{1,0:T(8,128)} %pad.9.cot_in, ...), custom_call_target="tpu_custom_call" | custom-call | flops 6000000000 | bytes 12000000 | tf_op jit(solution)/shard_map/critic/pallas_call | solution.py:367
  86.2 0.0 copy-start.1
  86.2 1.3 %slice_bitcast_fusion = f32[64]{0:T(128)} fusion(f32[8,128]{1,0:T(8,128)} %get-tuple-element.10), kind=kLoop, calls=%fused_computation.8 | loop fusion | bytes 512 | tf_op jit(solution)/shard_map/squeeze | solution.py:416
  87.6 0.0 copy-done.2
  87.6 0.8 slice_reduce_fusion
  88.4 1.5 %multiply_convert_fusion = bf16[1792,512]{1,0:T(8,128)(2,1)} fusion(f32[512]{0:T(512)S(1)} %convert_element_type.8, f32[1792]{0:T(1024)S(1)} %mul.15), kind=kLoop, calls=%fused_computation | loop fusion | flops 1835008 | bytes 1844224 | tf_op jit(solution)/shard_map/convert_element_type | solution.py:414
  90.0 1.5 %copy.19 = bf16[4,8192]{1,0:T(4,128)(2,1)} copy(bf16[4,8192]{1,0:T(4,128)(2,1)} %bitcast.14) | data formatting | bytes 131072
  91.5 0.0 copy-done.1
  91.5 0.0 copy-start
  91.5 1.2 %copy.20 = bf16[512,1792]{1,0:T(8,128)(2,1)} copy(bf16[512,1792]{1,0:T(8,128)(2,1)S(1)} %copy-done.1) | data formatting | bytes 3670016
  92.7 0.9 copy-done
  93.6 1.2 %copy.21 = bf16[512,1792]{1,0:T(8,128)(2,1)} copy(bf16[512,1792]{1,0:T(8,128)(2,1)S(1)} %copy-done) | data formatting | bytes 3670016
  (3 shorter events, 0.0 us)
Async XLA Ops:
  9.4 78.1 %copy-start.2 = (bf16[512]{0:T(512)(128)(2,1)S(1)}, bf16[512]{0:T(512)(128)(2,1)}, u32[]{:S(2)}) copy-start(bf16[512]{0:T(512)(128)(2,1)} %param.13) | copy-start | bytes 3076
  86.2 5.2 %copy-start.1 = (bf16[512,1792]{1,0:T(8,128)(2,1)S(1)}, bf16[512,1792]{1,0:T(8,128)(2,1)}, u32[]{:S(2)}) copy-start(bf16[512,1792]{1,0:T(8,128)(2,1)} %get-tuple-element.26) | copy-start | bytes 5505028
  91.5 2.2 %copy-start = (bf16[512,1792]{1,0:T(8,128)(2,1)S(1)}, bf16[512,1792]{1,0:T(8,128)(2,1)}, u32[]{:S(2)}) copy-start(bf16[512,1792]{1,0:T(8,128)(2,1)} %get-tuple-element.27) | copy-start | bytes 5505028

commit v3 on v1

v3 whole, which is shorter than its diff:
```python
import functools

import jax
import jax.numpy as jnp
from jax import lax
from jax.experimental import pallas as pl
from jax.experimental.pallas import tpu as pltpu
from jax.sharding import PartitionSpec as P

BF = jnp.bfloat16
F32 = jnp.float32
MESH = pl.DeviceIdType.MESH
HALF = 896
CHUNKS = 2
ROWS = 64
PART = ROWS // CHUNKS
CUTS = ((0, 640, 1280, 2 * HALF), (0, 512, 1152, 2 * HALF), (0, 640, 1152, 2 * HALF), (0, 640, 1280, 2 * HALF))


def dot(a, b):
    return jnp.dot(a, b, preferred_element_type=F32)


def dot_t(a, b):
    return lax.dot_general(a, b, (((1,), (1,)), ((), ())), preferred_element_type=F32)


def iota(shape, dim):
    return lax.broadcasted_iota(jnp.int32, shape, dim)


def xor(value, k, width):
    out = 0
    for b in range(width):
        bit = (value // (1 << b)) % 2
        out = out + ((1 - bit) if (k >> b) & 1 else bit) * (1 << b)
    return out


def kernel(
    x_hbm, order_hbm, head_hbm, cot_hbm, gate_w, up_w, down_w,
    gate_out, up_out, down_out, score_out, rows_out,
    x_in, order_in, head_in, cot_in, xs, xp, wb, down_v, place, rs, rb, lb, cot_own, cot_got, a_send, a_got, b_send, b_got,
    z_send, z_got, z_own, t_got, s_send, s_got, g_sib, d_send,
    x_s, x_r, cot_s, cot_r, xf_s, xf_r, w_s, w_r, loc, rs_s, rs_r, a_s, a_r, ag_s, ag_r, b_s, b_r,
    z_s, z_r, t_s, t_r, sc_s, sc_r, g_s, g_r, d_s, d_r,
):
    i = lax.axis_index("dp")
    j = lax.axis_index("tensor")
    core = i % 2
    x = (i // 2) % 4
    y = i // 8
    bits = (((x + 1) // 2) % 2, x // 2, y)
    block = bits[0] + 2 * bits[1] + 4 * bits[2]
    sib = (i + 1 - 2 * core, j)
    near = (
        (y * 8 + (x + 1 - 2 * (x % 2)) * 2 + core, j),
        (y * 8 + (3 - x) * 2 + core, j),
        ((1 - y) * 8 + x * 2 + core, j),
    )
    t_peer = [None] + [(i, xor(j, k, 3)) for k in range(1, 8)]
    d_peer = [None] + [(xor(i, k, 4), j) for k in range(1, 16)]
    sent = []

    def remote(src, dst, send, recv, device):
        copy = pltpu.make_async_remote_copy(
            src_ref=src, dst_ref=dst, send_sem=send, recv_sem=recv, device_id=device, device_id_type=MESH
        )
        copy.start()
        sent.append(copy)
        return copy

    mine = pl.ds(pl.multiple_of(core * HALF, 128), HALF)
    other = pl.ds(pl.multiple_of((1 - core) * HALF, 128), HALF)
    gates, ups = pl.ds(0, HALF), pl.ds(HALF, HALF)

    barrier = pltpu.get_barrier_semaphore()
    far = (6, 5, 7, 4, 2, 1, 3)
    for device in [t_peer[k] for k in far] + d_peer[:0:-1]:
        pl.semaphore_signal(barrier, inc=1, device_id=device, device_id_type=MESH)
    local = [
        pltpu.make_async_copy(down_w, down_v, loc.at[0]),
        pltpu.make_async_copy(gate_w.at[:, mine], wb.at[0, :, gates], loc.at[1]),
        pltpu.make_async_copy(up_w.at[:, mine], wb.at[0, :, ups], loc.at[2]),
    ]
    small = [
        pltpu.make_async_copy(x_hbm, x_in, loc.at[3]),
        pltpu.make_async_copy(order_hbm, order_in, loc.at[4]),
        pltpu.make_async_copy(head_hbm, head_in, loc.at[5]),
        pltpu.make_async_copy(cot_hbm, cot_in, loc.at[6]),
    ]
    for copy in small + local:
        copy.start()
    for copy in small:
        copy.wait()
    spot = iota((8, 128), 0) * 128 + iota((8, 128), 1) - (32 * i + 4 * j)
    cot_tile = jnp.zeros((8, 128), F32)
    for r in range(4):
        cot_tile = jnp.where(spot == r, cot_in[r], cot_tile)
    cot_own[...] = cot_tile
    pl.semaphore_wait(barrier, 22)
    x_copies = {k: remote(x_in, xs.at[0, j], x_s.at[k], x_r.at[k], t_peer[k]) for k in far}
    forward = [remote(x_in, xs.at[1, j], xf_s.at[0], xf_r.at[0], sib)]
    w_copies = [
        remote(gate_w.at[:, other], wb.at[1, :, gates], w_s.at[0], w_r.at[0], sib),
        remote(up_w.at[:, other], wb.at[1, :, ups], w_s.at[1], w_r.at[1], sib),
    ]
    cot_copies = [remote(cot_own, cot_got.at[k], cot_s.at[k], cot_r.at[k], t_peer[k]) for k in far]
    xs[0, pl.ds(j, 1)] = x_in[...][None]
    head_row = head_in[...].reshape(1, 512)
    order_row = order_in[...].reshape(1, 512)
    head_rows = jnp.broadcast_to(head_row, (16, 512))
    x_head = dot_t(head_rows, x_in[...])
    local[0].wait()
    a_send[...] = jnp.zeros_like(a_send)
    a_send[0, 0:1, :] = dot_t(head_rows, down_v[mine, :])[0:1]
    a_send[1, 0:1, :] = dot_t(head_rows, down_v[other, :])[0:1]
    for v in range(2):
        a_send[v, 1:2, 0:ROWS] = x_head[0:1]
    n = iota((512, 512), 0)
    hot = (n == jnp.broadcast_to(order_row, (512, 512))).astype(BF)
    turn = iota((512, 512), 1) == 32 * ((n // 4) % 16) + 4 * (n // 64) + n % 4
    place[...] = dot_t(turn.astype(BF), hot).astype(BF)
    for k in (1, 3, 2, 4, 5, 7, 6):
        x_copies[k].wait_recv()
        there = xor(j, k, 3)
        forward.append(remote(xs.at[0, there], xs.at[1, there], xf_s.at[k], xf_r.at[k], sib))
    def permute(v):
        for c in (0, 256):
            xp[v, :, c:c + 256] = dot(place[...], xs[v, :, :, c:c + 256].reshape(512, 256)).astype(BF)

    permute(0)
    for copy in local[1:]:
        copy.wait()
    for copy in forward + w_copies:
        copy.wait_recv()
    permute(1)
    def view(h, p, fixed, flip=None):
        where = [pl.ds(0, 2)] * 3
        for d in fixed:
            where[2 - d] = pl.ds(bits[d], 1)
        if flip is not None:
            where[2 - flip] = pl.ds(1 - bits[flip], 1)
        return (h, *where, slice(None), pl.ds(CUTS[h][p], CUTS[h][p + 1] - CUTS[h][p]))

    def dims(p):
        return [p, (p + 1) % 3, (p + 2) % 3]

    rs_copies, ag_copies = {}, {}

    def rs_start(h, p, s):
        order = dims(p)
        part = view(h, p, order[:s], order[s])
        k = 9 * h + 3 * p + s
        rs_copies[h, p, s] = remote(rs.at[part], rb.at[(s, *part)], rs_s.at[k], rs_r.at[k], near[order[s]])

    def ag_start(h, p, s):
        order = dims(p)
        part = view(h, p, order[:3 - s])
        k = 9 * h + 3 * p + s
        ag_copies[h, p, s] = remote(lb.at[part], lb.at[part], ag_s.at[k], ag_r.at[k], near[order[2 - s]])

    def x_part(v, h):
        rows = [xp[v, b * ROWS + h * PART:b * ROWS + (h + 1) * PART, :] for b in range(8)]
        return jnp.concatenate(rows, axis=0)

    for h in range(CHUNKS):
        x_own, x_sib = x_part(0, h), x_part(1, h)
        done = 0
        for lo in range(0, 2 * HALF, 256):
            cols = slice(lo, lo + 256)
            part = dot(x_own, wb[0, :, cols]) + dot(x_sib, wb[1, :, cols])
            rs[h, :, :, :, :, cols] = part.astype(BF).reshape(2, 2, 2, PART, 256)
            while done < 3 and lo + 256 >= CUTS[h][done + 1]:
                rs_start(h, done, 0)
                done += 1
        if h == 0:
            for copy in cot_copies:
                copy.wait_recv()
            for k in range(1, 8):
                cot_tile = cot_tile + cot_got[k]
            for v in range(2):
                a_send[v, 4:8, 0:128] = cot_tile[0:4]
            a_copies = [remote(a_send.at[1], a_got.at[0], a_s.at[0], a_r.at[0], sib)]
        if h == 1:
            a_copies[0].wait_recv()
            a_send[2] = a_send[0] + a_got[0]
            a_copies.append(remote(a_send.at[2], a_got.at[1], a_s.at[1], a_r.at[1], near[0]))

    def rs_add(h, p, s, own):
        order = dims(p)
        if own:
            part = view(h, p, order[:s + 2])
        else:
            part = view(h, p, order[:s + 1], order[s + 1])
        rs[part] = (rs[part].astype(F32) + rb[(s, *part)].astype(F32)).astype(BF)

    for s in range(2):
        for h in range(CHUNKS):
            for p in range(3):
                rs_copies[h, p, s].wait_recv()
                rs_add(h, p, s, False)
                rs_start(h, p, s + 1)
            for p in range(3):
                rs_add(h, p, s, True)
        a_copies[s + 1].wait_recv()
        a_send[s + 3] = a_send[s + 2] + a_got[s + 1]
        a_copies.append(remote(a_send.at[s + 3], a_got.at[s + 2], a_s.at[s + 2], a_r.at[s + 2], near[s + 1]))
    a_copies[3].wait_recv()
    a_sum = a_send[4] + a_got[3]
    unit_head = a_sum[0:1, :]
    cots = a_sum[4:8, 0:128]
    lanes, subs = iota((PART, 128), 1), iota((PART, 128), 0)

    def cot_rows(owner, h):
        train_k = 32 * ((subs + h * PART) // 4) + 4 * owner + subs % 4
        total = jnp.zeros((PART, 128), F32)
        for r in range(4):
            row = jnp.broadcast_to(cots[r:r + 1], (PART, 128))
            total = total + jnp.where(lanes + 128 * r == train_k, row, 0.0)
        return jnp.sum(total, axis=1, keepdims=True)

    sub8 = iota((8, 128), 0)
    vec = jnp.zeros((1, HALF), F32)
    score = jnp.zeros((1, 128), F32)
    for h in range(CHUNKS):
        cot_here = cot_rows(block, h)
        back = cot_here * unit_head
        summed = []
        for p in range(3):
            rs_copies[h, p, 2].wait_recv()
            part = view(h, p, (0, 1, 2))
            width = CUTS[h][p + 1] - CUTS[h][p]
            summed.append((rs[part].astype(F32) + rb[(2, *part)].astype(F32)).reshape(PART, width))
        summed = jnp.concatenate(summed, axis=1)
        gate, up = summed[:, 0:HALF], summed[:, HALF:2 * HALF]
        sig = jax.nn.sigmoid(gate)
        swish = gate * sig
        gate_low = (back * up * sig * (1.0 + gate * (1.0 - sig))).astype(BF)
        up_low = (back * swish).astype(BF)
        spot = (h, pl.ds(bits[2], 1), pl.ds(bits[1], 1), pl.ds(bits[0], 1), slice(None))
        lb[(*spot, gates)] = gate_low.reshape(1, 1, 1, PART, HALF)
        lb[(*spot, ups)] = up_low.reshape(1, 1, 1, PART, HALF)
        for p in range(3):
            ag_start(h, p, 0)
        hidden = (swish * up).astype(BF).astype(F32)
        vec = vec + jnp.sum(hidden * cot_here, axis=0, keepdims=True)
        score_col = jnp.sum(hidden * unit_head, axis=1, keepdims=True)
        spot = lanes == subs + h * PART + ROWS * (block % 2)
        score = score + jnp.sum(jnp.where(spot, score_col, 0.0), axis=0, keepdims=True)

    b_send[...] = jnp.zeros_like(b_send)
    b_send[0, 0:1, :] = vec
    b_send[0, 8:16, 0:128] = jnp.where(sub8 == block // 2, score, 0.0)
    b_copies = [remote(b_send.at[0], b_got.at[0], b_s.at[0], b_r.at[0], near[0])]
    for s in range(2):
        for h in range(CHUNKS):
            for p in range(3):
                ag_copies[h, p, s].wait_recv()
                ag_start(h, p, s + 1)
        b_copies[s].wait_recv()
        b_send[s + 1] = b_send[s] + b_got[s]
        b_copies.append(remote(b_send.at[s + 1], b_got.at[s + 1], b_s.at[s + 1], b_r.at[s + 1], near[s + 1]))
    def low(h):
        return lb[h].reshape(8 * PART, 2 * HALF)

    z_copies, t_copies = [], {}
    for h in range(CHUNKS):
        for p in range(3):
            ag_copies[h, p, 2].wait_recv()
        for c in (0, 256):
            z_send[h, :, c:c + 256] = dot_t(low(h), wb[1, c:c + 256, :]).astype(BF)
        z_copies.append(remote(z_send.at[h], z_got.at[h], z_s.at[h], z_r.at[h], sib))
        own = [dot_t(low(h), wb[0, c:c + 256, :]) for c in (0, 256)]
        z_copies[h].wait_recv()
        for n, c in enumerate((0, 256)):
            both = own[n] + z_got[h, :, c:c + 256].astype(F32)
            z_own[h, :, :, c:c + 256] = both.astype(BF).reshape(8, PART, 256)
        for k in far:
            t_copies[h, k] = remote(
                z_own.at[h, xor(j, k, 3)], t_got.at[h, k], t_s.at[8 * h + k], t_r.at[8 * h + k], t_peer[k]
            )
        if h == 0:
            b_copies[2].wait_recv()
            b_send[3] = b_send[2] + b_got[2]
            b_copies.append(remote(b_send.at[3], b_got.at[3], b_s.at[3], b_r.at[3], sib))
    b_copies[3].wait_recv()
    s_send[...] = b_send[3, 8:16, 0:128] + b_got[3, 8:16, 0:128]
    sc_copies = [remote(s_send, s_got.at[k], sc_s.at[k], sc_r.at[k], t_peer[k]) for k in range(1, 8)]
    def grad(v, lo, width):
        total = jnp.zeros((512, width), F32)
        for h in range(CHUNKS):
            lows = lb[h, :, :, :, :, lo:lo + width].reshape(8 * PART, width)
            total = total + lax.dot_general(
                x_part(v, h), lows, (((0,), (0,)), ((), ())), preferred_element_type=F32
            )
        return total.astype(BF)

    for lo in range(0, 2 * HALF, 256):
        g_sib[:, lo:lo + 256] = grad(1, lo, 256)
    g_copies = [
        remote(g_sib.at[:, gates], gate_out.at[:, mine], g_s.at[0], g_r.at[0], sib),
        remote(g_sib.at[:, ups], up_out.at[:, mine], g_s.at[1], g_r.at[1], sib),
    ]
    for first, out in ((0, gate_out), (HALF, up_out)):
        for lo, width in ((0, 256), (256, 256), (512, 256), (768, 128)):
            where = pl.ds(pl.multiple_of(core * HALF + lo, 128), width)
            out[:, where] = grad(0, first + lo, width)

    want, have = iota((4 * PART, 4 * PART), 0), iota((4 * PART, 4 * PART), 1)
    source = ((want // 4) % 4) * PART + (want // 16) * 4 + want % 4
    gather = (have == source).astype(BF)
    each = 16 // CHUNKS
    seat = i % each

    def d_copy(h, k):
        there = each * h + xor(seat, k, 3)
        return pltpu.make_async_remote_copy(
            src_ref=d_send.at[there], dst_ref=rows_out.at[i],
            send_sem=d_s.at[each * h + k], recv_sem=d_r.at[each * (i // each) + k],
            device_id=(there, j), device_id_type=MESH,
        )

    for h in range(CHUNKS):
        total = z_own[h, pl.ds(j, 1)].reshape(PART, 512).astype(F32)
        for k in far:
            t_copies[h, k].wait_recv()
            total = total + t_got[h, k].astype(F32)
        low_rows = (total + cot_rows(j, h) * head_row.astype(F32)).astype(BF)
        stacked = jnp.concatenate([low_rows[:, c:c + 128] for c in range(0, 512, 128)], axis=0)
        d_send[each * h:each * (h + 1)] = dot(gather, stacked).astype(BF).reshape(each, 16, 128)
        for k in range(each - 1, -1, -1):
            if k:
                d_copy(h, k).start()
            else:
                pl.when(i // each != h)(d_copy(h, 0).start)
    rows_out[pl.ds(i, 1)] = d_send[pl.ds(i, 1)]

    score = s_send[...]
    for k in range(1, 8):
        sc_copies[k - 1].wait_recv()
        score = score + s_got[k]
    score = jnp.concatenate([score[r:r + 1] for r in range(4)], axis=1)
    high = score.astype(BF)
    rest = score - high.astype(F32)
    middle = rest.astype(BF)
    last = (rest - middle.astype(F32)).astype(BF)
    split = jnp.concatenate([high, middle, last, jnp.zeros((13, 512), BF)], axis=0)
    moved = dot(split, place[...])
    moved = moved[0:1] + moved[1:2] + moved[2:3]
    score = a_sum[1:2, 0:ROWS]
    for b in range(8):
        score = score + jnp.where(j == b, moved[:, b * ROWS:(b + 1) * ROWS], 0.0)
    score_out[...] = jnp.zeros_like(score_out)
    score_out[0:1, 0:ROWS] = score
    head_float = head_row.astype(F32)
    for v, source in ((core, b_send), (1 - core, b_got)):
        for c in range(0, HALF, 128):
            column = jnp.broadcast_to(source[3, 0:1, c:c + 128], (128, 128)).T
            rows = pl.ds(pl.multiple_of(v * HALF + c, 128), 128)
            down_out[rows, :] = (jnp.concatenate([column] * 4, axis=1) * head_float).astype(BF)
    for half in range(CHUNKS):
        for k in range(each):
            got = pltpu.make_async_remote_copy(
                src_ref=d_send.at[0], dst_ref=rows_out.at[each * half + xor(seat, k, 3)],
                send_sem=d_s.at[0], recv_sem=d_r.at[each * half + k],
                device_id=sib, device_id_type=MESH,
            )
            if k:
                got.wait_recv()
                d_copy(half, k).wait_send()
            else:
                pl.when(i // each != half)(got.wait_recv)
                pl.when(i // each != half)(d_copy(half, 0).wait_send)
    for copy in g_copies:
        copy.wait_recv()
    for copy in sent:
        copy.wait_send()


def finish_kernel(gate_in, up_in, down_in, score_in, rows_in, gate_out, up_out, down_out, score_out, rows_out, sem):
    copies = [
        pltpu.make_async_copy(gate_in, gate_out, sem.at[0]),
        pltpu.make_async_copy(up_in, up_out, sem.at[1]),
        pltpu.make_async_copy(down_in, down_out, sem.at[2]),
    ]
    for copy in copies:
        copy.start()
    score_out[...] = score_in[0:1, 0:ROWS].reshape(ROWS)
    rows = rows_in[...].astype(F32).reshape(256, 128)
    rows_out[...] = jnp.concatenate([rows[4 * n:4 * n + 4] for n in range(64)], axis=1).astype(BF)
    for copy in copies:
        copy.wait()


def per_device(inputs, ordering, cotangent, gate_weight, up_weight, down_weight, value_head):
    whole = pl.BlockSpec(memory_space=pl.ANY)
    held = pl.BlockSpec(memory_space=pltpu.VMEM)
    dma = pltpu.SemaphoreType.DMA
    cube = (CHUNKS, 2, 2, 2, PART, 2 * HALF)
    gate_grad, up_grad, down_grad, score, rows = pl.pallas_call(
        kernel,
        name="critic",
        out_shape=(
            pltpu.VMEM((512, 2 * HALF), BF),
            pltpu.VMEM((512, 2 * HALF), BF),
            pltpu.VMEM((2 * HALF, 512), BF),
            pltpu.VMEM((8, 128), F32),
            pltpu.VMEM((16, 16, 128), BF),
        ),
        in_specs=[whole] * 7,
        out_specs=(held,) * 5,
        scratch_shapes=[
            pltpu.VMEM((ROWS, 512), BF),
            pltpu.VMEM((512,), jnp.int32),
            pltpu.VMEM((512,), BF),
            pltpu.SMEM((4,), F32),
            pltpu.VMEM((2, 8, ROWS, 512), BF),
            pltpu.VMEM((2, 512, 512), BF),
            pltpu.VMEM((2, 512, 2 * HALF), BF),
            pltpu.VMEM((2 * HALF, 512), BF),
            pltpu.VMEM((512, 512), BF),
            pltpu.VMEM(cube, BF),
            pltpu.VMEM((3, *cube), BF),
            pltpu.VMEM(cube, BF),
            pltpu.VMEM((8, 128), F32),
            pltpu.VMEM((8, 8, 128), F32),
            pltpu.VMEM((5, 8, HALF), F32),
            pltpu.VMEM((4, 8, HALF), F32),
            pltpu.VMEM((4, 16, HALF), F32),
            pltpu.VMEM((4, 16, HALF), F32),
            pltpu.VMEM((CHUNKS, 8 * PART, 512), BF),
            pltpu.VMEM((CHUNKS, 8 * PART, 512), BF),
            pltpu.VMEM((CHUNKS, 8, PART, 512), BF),
            pltpu.VMEM((CHUNKS, 8, PART, 512), BF),
            pltpu.VMEM((8, 128), F32),
            pltpu.VMEM((8, 8, 128), F32),
            pltpu.VMEM((512, 2 * HALF), BF),
            pltpu.VMEM((16, 16, 128), BF),
            *[dma((8,))] * 6, dma((2,)), dma((2,)), dma((7,)), dma((9 * CHUNKS,)), dma((9 * CHUNKS,)),
            dma((4,)), dma((4,)), dma((9 * CHUNKS,)), dma((9 * CHUNKS,)), dma((4,)), dma((4,)),
            dma((CHUNKS,)), dma((CHUNKS,)), dma((8 * CHUNKS,)), dma((8 * CHUNKS,)), dma((8,)), dma((8,)), dma((2,)), dma((2,)), dma((16,)), dma((16,)),
        ],
        compiler_params=pltpu.CompilerParams(
            collective_id=0, has_side_effects=True, vmem_limit_bytes=44 * 2**20
        ),
        cost_estimate=pl.CostEstimate(flops=6 * 10**9, bytes_accessed=12 * 10**6, transcendentals=10**5),
    )(*[
        pltpu.with_memory_space_constraint(a, pltpu.HBM)
        for a in (inputs, ordering, value_head, cotangent, gate_weight, up_weight, down_weight)
    ])
    score, rows, gate_grad, up_grad, down_grad = finish_call(gate_grad, up_grad, down_grad, score, rows)
    return (score, rows, gate_grad, up_grad, down_grad)


def finish_call(gate_grad, up_grad, down_grad, score, rows):
    whole = pl.BlockSpec(memory_space=pl.ANY)
    held = pl.BlockSpec(memory_space=pltpu.VMEM)
    outs = pl.pallas_call(
        finish_kernel,
        name="deliver",
        out_shape=(
            jax.ShapeDtypeStruct((512, 2 * HALF), BF),
            jax.ShapeDtypeStruct((512, 2 * HALF), BF),
            jax.ShapeDtypeStruct((2 * HALF, 512), BF),
            jax.ShapeDtypeStruct((ROWS,), F32),
            jax.ShapeDtypeStruct((4, 8192), BF),
        ),
        in_specs=[whole] * 3 + [held] * 2,
        out_specs=(whole,) * 3 + (held,) * 2,
        scratch_shapes=[pltpu.SemaphoreType.DMA((3,))],
        compiler_params=pltpu.CompilerParams(vmem_limit_bytes=8 * 2**20),
    )(gate_grad, up_grad, down_grad, score, rows)
    return outs[3], outs[4], outs[0], outs[1], outs[2]


def solution(mesh):
    placed = (
        P("tensor", "dp"),
        P(),
        P(("dp", "tensor")),
        P("dp", "tensor"),
        P("dp", "tensor"),
        P("tensor", "dp"),
        P("dp"),
    )
    return jax.shard_map(
        per_device,
        mesh=mesh,
        in_specs=placed,
        out_specs=(
            P("tensor"),
            P(("dp", "tensor"), None),
            P("dp", "tensor"),
            P("dp", "tensor"),
            P("tensor", "dp"),
        ),
        check_vma=False,
    )
```

time: 349 us -> 70.4 us (0.20)
  blocking collectives: 223 us -> 0 us
  Pallas kernels: 0 us -> 69.6 us
  waiting for transfers between devices: 59 us -> 0 us
  local copies, waits for them, and re-layouts: 22.9 us -> 0 us
  matrix products: 13.4 us -> 0 us
  between operations: 13.9 us -> 0.64 us
  starting transfers between devices: 8.05 us -> 0 us
  other arithmetic: 6.28 us -> 0 us
    psum x3 -> x0, blocking collectives: 121 us -> none  [the longest x1 64 us: per_device(): score = lax.psum(score, ('dp', 'tensor'))]
    unnamed x1 -> x0, blocking collectives: 71.9 us -> none
    pallas_call x0 -> x2, Pallas kernels: none -> 69.6 us  [the longest x1 66.5 us: per_device(): pl.pallas_call(kernel, name='critic', out_shape=(pltpu.VMEM((512, 2 * HAL...]
    reduce_scatter x2 -> x0, waiting for transfers between devices: 56.3 us -> none  [the longest x1 56.3 us: per_device(): lax.psum_scatter(part, 'tensor', scatter_dimension=0, tiled=True)]
    all_gather x1 -> x0, blocking collectives: 29.9 us -> none  [per_device(): columns = lax.all_gather(inputs, 'tensor', axis=0, tiled=True)]
    unnamed x20 -> x0, local copies, waits for them, and re-layouts: 17.1 us -> none
    dot_general x3 -> x0, matrix products: 13.4 us -> none  [the longest x1 5.24 us: per_device(): lax.dot_general(low, both_weight, (((1,), (1,)), ((), ())), preferred_ele...]
    all_to_all x1 -> x0, starting transfers between devices: 7.93 us -> none  [per_device(): lax.all_to_all(input_rows, 'dp', split_axis=0, concat_axis=1, tiled=True)]
  transfers between devices with their start and end apart: 4 -> 0, of which waited for: 2 -> 0; matrix products, arithmetic and copies ran while one was open for 5% -> 0% of each run, Pallas kernels for 0% -> 0%
where the time goes in v3:
time: 70.4 us; the launch traced here: 70.3 us
  Pallas kernels  69.6 us (99%)
    pallas_call x1, Pallas kernels, per_device(): pl.pallas_call(kernel, name='critic', out_shape=(pltpu.VMEM((512, 2 * HAL...  66.5 us
    pallas_call x1, Pallas kernels, finish_call(): pl.pallas_call(finish_kernel, name='deliver', out_shape=(jax.ShapeDtypeSt...  3.1 us

profile of v3, /device:TPU:9, one launch (start us, length us, event | category | flops | bytes accessed | tf_op | source)
XLA Modules:
  0.0 70.3 jit_solution(2673822735849342866)
XLA Ops:
  0.6 66.5 %critic.1 = (bf16[512,1792]{1,0:T(8,128)(2,1)S(1)}, bf16[512,1792]{1,0:T(8,128)(2,1)S(1)}, bf16[1792,512]{1,0:T(8,128)(2,1)S(1)}, f32[8,128]{1,0:T(8,128)S(1)}, bf16[16,16,128]{2,1,0:T(8,128)(2,1)S(1)}) custom-call(bf16[64,512]{1,0:T(8,128)(2,1)} %x_hbm.1, s32[512]{0:T(512)} %order_hbm.1, bf16[512]{0:T(512)(128)(2,1)} %head_hbm.1, f32[4]{0:T(128)} %cot_hbm.1, ...), custom_call_target="tpu_custom_call" | custom-call | flops 6000000000 | bytes 12000000 | tf_op jit(solution)/shard_map/critic/pallas_call | solution.py:401
  67.2 3.1 %deliver.1 = (bf16[512,1792]{1,0:T(8,128)(2,1)}, bf16[512,1792]{1,0:T(8,128)(2,1)}, bf16[1792,512]{1,0:T(8,128)(2,1)}, f32[64]{0:T(128)}, bf16[4,8192]{1,0:T(4,128)(2,1)}) custom-call(bf16[512,1792]{1,0:T(8,128)(2,1)S(1)} %get-tuple-element.15.gate_in, bf16[512,1792]{1,0:T(8,128)(2,1)S(1)} %get-tuple-element.16.up_in, ...), custom_call_target="tpu_custom_call" | custom-call | tf_op jit(solution)/shard_map/deliver/pallas_call | solution.py:459

commit v4 on v3

--- a/solution.py
+++ b/solution.py
@@ -12,6 +12,10 @@
 MESH = pl.DeviceIdType.MESH
 HALF = 896
 CHUNKS = 2
+ROWS = 64
+PART = ROWS // CHUNKS
+CHUNKS = 2
+STEP, SHIFT = 3.0, 1.1
 ROWS = 64
 PART = ROWS // CHUNKS
 CUTS = ((0, 640, 1280, 2 * HALF), (0, 512, 1152, 2 * HALF), (0, 640, 1152, 2 * HALF), (0, 640, 1280, 2 * HALF))
@@ -53,11 +57,24 @@
     bits = (((x + 1) // 2) % 2, x // 2, y)
     block = bits[0] + 2 * bits[1] + 4 * bits[2]
     sib = (i + 1 - 2 * core, j)
-    near = (
-        (y * 8 + (x + 1 - 2 * (x % 2)) * 2 + core, j),
-        (y * 8 + (3 - x) * 2 + core, j),
-        ((1 - y) * 8 + x * 2 + core, j),
-    )
+
+    def flip(*turned):
+        at = x
+        if 0 in turned:
+            at = at + 1 - 2 * (at % 2)
+        if 1 in turned:
+            at = 3 - at
+        return (((1 - y) if 2 in turned else y) * 8 + at * 2 + core, j)
+
+    near = (flip(0), flip(1), flip(2))
+    chips = [flip(0, 1, 2), flip(0, 1), flip(0, 2), flip(1, 2), flip(2), flip(1), flip(0)]
+
+    def fold(row):
+        return jnp.concatenate([row[:, c:c + 128] for c in range(0, HALF, 128)], axis=0)
+
+    def unfold(tile):
+        return jnp.concatenate([tile[r:r + 1] for r in range(HALF // 128)], axis=1)
+
     t_peer = [None] + [(i, xor(j, k, 3)) for k in range(1, 8)]
     d_peer = [None] + [(xor(i, k, 4), j) for k in range(1, 16)]
     sent = []
@@ -99,13 +116,13 @@
         cot_tile = jnp.where(spot == r, cot_in[r], cot_tile)
     cot_own[...] = cot_tile
     pl.semaphore_wait(barrier, 22)
+    cot_copies = [remote(cot_own, cot_got.at[k], cot_s.at[k], cot_r.at[k], t_peer[k]) for k in far]
     x_copies = {k: remote(x_in, xs.at[0, j], x_s.at[k], x_r.at[k], t_peer[k]) for k in far}
     forward = [remote(x_in, xs.at[1, j], xf_s.at[0], xf_r.at[0], sib)]
     w_copies = [
         remote(gate_w.at[:, other], wb.at[1, :, gates], w_s.at[0], w_r.at[0], sib),
         remote(up_w.at[:, other], wb.at[1, :, ups], w_s.at[1], w_r.at[1], sib),
     ]
-    cot_copies = [remote(cot_own, cot_got.at[k], cot_s.at[k], cot_r.at[k], t_peer[k]) for k in far]
     xs[0, pl.ds(j, 1)] = x_in[...][None]
     head_row = head_in[...].reshape(1, 512)
     order_row = order_in[...].reshape(1, 512)
@@ -113,58 +130,113 @@
     x_head = dot_t(head_rows, x_in[...])
     local[0].wait()
     a_send[...] = jnp.zeros_like(a_send)
-    a_send[0, 0:1, :] = dot_t(head_rows, down_v[mine, :])[0:1]
-    a_send[1, 0:1, :] = dot_t(head_rows, down_v[other, :])[0:1]
+    a_send[0, 0:7, :] = fold(dot_t(head_rows, down_v[mine, :])[0:1])
+    a_send[1, 0:7, :] = fold(dot_t(head_rows, down_v[other, :])[0:1])
     for v in range(2):
-        a_send[v, 1:2, 0:ROWS] = x_head[0:1]
+        a_send[v, 7:8, 0:ROWS] = x_head[0:1]
     n = iota((512, 512), 0)
     hot = (n == jnp.broadcast_to(order_row, (512, 512))).astype(BF)
     turn = iota((512, 512), 1) == 32 * ((n // 4) % 16) + 4 * (n // 64) + n % 4
     place[...] = dot_t(turn.astype(BF), hot).astype(BF)
+    a_copies, b_copies = [], []
+
+    def a_first():
+        for copy in cot_copies:
+            copy.wait_recv()
+        total = cot_tile
+        for k in range(1, 8):
+            total = total + cot_got[k]
+        for v in range(2):
+            a_send[v, 8:12, :] = total[0:4]
+        a_copies.append(remote(a_send.at[1], a_got.at[7], a_s.at[7], a_r.at[7], sib))
+
+    def a_second():
+        a_copies[0].wait_recv()
+        a_send[2] = a_send[0] + a_got[7]
+        for n, device in enumerate(chips):
+            a_copies.append(remote(a_send.at[2], a_got.at[n], a_s.at[n], a_r.at[n], device))
+
+    def a_last():
+        total = a_send[2]
+        for n in range(7):
+            a_copies[n + 1].wait_recv()
+            total = total + a_got[n]
+        return total
+
+    def b_first(vec, score):
+        b_send[0, 0:7, :] = fold(vec)
+        b_send[0, 7:8, :] = jnp.zeros((1, 128), F32)
+        b_send[0, 8:16, :] = jnp.where(sub8 == block // 2, score, 0.0)
+        for n, device in enumerate(chips):
+            b_copies.append(remote(b_send.at[0], b_got.at[n], b_s.at[n], b_r.at[n], device))
+
+    def b_second():
+        total = b_send[0]
+        for n in range(7):
+            b_copies[n].wait_recv()
+            total = total + b_got[n]
+        b_send[1] = total
+        b_copies.append(remote(b_send.at[1], b_got.at[7], b_s.at[7], b_r.at[7], sib))
+
     for k in (1, 3, 2, 4, 5, 7, 6):
         x_copies[k].wait_recv()
         there = xor(j, k, 3)
         forward.append(remote(xs.at[0, there], xs.at[1, there], xf_s.at[k], xf_r.at[k], sib))
+
     def permute(v):
         for c in (0, 256):
             xp[v, :, c:c + 256] = dot(place[...], xs[v, :, :, c:c + 256].reshape(512, 256)).astype(BF)
 
     permute(0)
+    a_first()
     for copy in local[1:]:
         copy.wait()
     for copy in forward + w_copies:
         copy.wait_recv()
     permute(1)
-    def view(h, p, fixed, flip=None):
+    a_second()
+    def view(h, p, fixed, turned=()):
         where = [pl.ds(0, 2)] * 3
         for d in fixed:
-            where[2 - d] = pl.ds(bits[d], 1)
-        if flip is not None:
-            where[2 - flip] = pl.ds(1 - bits[flip], 1)
+            where[2 - d] = pl.ds(1 - bits[d] if d in turned else bits[d], 1)
         return (h, *where, slice(None), pl.ds(CUTS[h][p], CUTS[h][p + 1] - CUTS[h][p]))
 
-    def dims(p):
-        return [p, (p + 1) % 3, (p + 2) % 3]
-
+    def turns(p):
+        b, c = (p + 1) % 3, (p + 2) % 3
+        return ((b, c), (b,), (c,))
+
+    every = (0, 1, 2)
     rs_copies, ag_copies = {}, {}
 
-    def rs_start(h, p, s):
-        order = dims(p)
-        part = view(h, p, order[:s], order[s])
-        k = 9 * h + 3 * p + s
-        rs_copies[h, p, s] = remote(rs.at[part], rb.at[(s, *part)], rs_s.at[k], rs_r.at[k], near[order[s]])
-
-    def ag_start(h, p, s):
-        order = dims(p)
-        part = view(h, p, order[:3 - s])
-        k = 9 * h + 3 * p + s
-        ag_copies[h, p, s] = remote(lb.at[part], lb.at[part], ag_s.at[k], ag_r.at[k], near[order[2 - s]])
+    def rs_first(h, p):
+        part = view(h, p, (p,), (p,))
+        k = 12 * h + 4 * p
+        rs_copies[h, p, 0] = remote(rs.at[part], rb.at[(0, *part)], rs_s.at[k], rs_r.at[k], near[p])
+
+    def rs_second(h, p):
+        for n, turned in enumerate(turns(p)):
+            part = view(h, p, every, turned)
+            k = 12 * h + 4 * p + n + 1
+            rs_copies[h, p, n + 1] = remote(
+                rs.at[part], rb.at[(n + 1, *part)], rs_s.at[k], rs_r.at[k], flip(*turned)
+            )
+
+    def ag_first(h, p):
+        part = view(h, p, every)
+        for n, turned in enumerate(turns(p)):
+            k = 12 * h + 4 * p + n + 1
+            ag_copies[h, p, n + 1] = remote(lb.at[part], lb.at[part], ag_s.at[k], ag_r.at[k], flip(*turned))
+
+    def ag_second(h, p):
+        part = view(h, p, (p,))
+        k = 12 * h + 4 * p
+        ag_copies[h, p, 0] = remote(lb.at[part], lb.at[part], ag_s.at[k], ag_r.at[k], near[p])
 
     def x_part(v, h):
         rows = [xp[v, b * ROWS + h * PART:b * ROWS + (h + 1) * PART, :] for b in range(8)]
         return jnp.concatenate(rows, axis=0)
 
-    for h in range(CHUNKS):
+    def products(h):
         x_own, x_sib = x_part(0, h), x_part(1, h)
         done = 0
         for lo in range(0, 2 * HALF, 256):
@@ -172,66 +244,46 @@
             part = dot(x_own, wb[0, :, cols]) + dot(x_sib, wb[1, :, cols])
             rs[h, :, :, :, :, cols] = part.astype(BF).reshape(2, 2, 2, PART, 256)
             while done < 3 and lo + 256 >= CUTS[h][done + 1]:
-                rs_start(h, done, 0)
+                rs_first(h, done)
                 done += 1
-        if h == 0:
-            for copy in cot_copies:
-                copy.wait_recv()
-            for k in range(1, 8):
-                cot_tile = cot_tile + cot_got[k]
-            for v in range(2):
-                a_send[v, 4:8, 0:128] = cot_tile[0:4]
-            a_copies = [remote(a_send.at[1], a_got.at[0], a_s.at[0], a_r.at[0], sib)]
-        if h == 1:
-            a_copies[0].wait_recv()
-            a_send[2] = a_send[0] + a_got[0]
-            a_copies.append(remote(a_send.at[2], a_got.at[1], a_s.at[1], a_r.at[1], near[0]))
-
-    def rs_add(h, p, s, own):
-        order = dims(p)
-        if own:
-            part = view(h, p, order[:s + 2])
-        else:
-            part = view(h, p, order[:s + 1], order[s + 1])
-        rs[part] = (rs[part].astype(F32) + rb[(s, *part)].astype(F32)).astype(BF)
-
-    for s in range(2):
-        for h in range(CHUNKS):
-            for p in range(3):
-                rs_copies[h, p, s].wait_recv()
-                rs_add(h, p, s, False)
-                rs_start(h, p, s + 1)
-            for p in range(3):
-                rs_add(h, p, s, True)
-        a_copies[s + 1].wait_recv()
-        a_send[s + 3] = a_send[s + 2] + a_got[s + 1]
-        a_copies.append(remote(a_send.at[s + 3], a_got.at[s + 2], a_s.at[s + 2], a_r.at[s + 2], near[s + 1]))
-    a_copies[3].wait_recv()
-    a_sum = a_send[4] + a_got[3]
-    unit_head = a_sum[0:1, :]
-    cots = a_sum[4:8, 0:128]
+
+    def halve(h):
+        for p in range(3):
+            rs_copies[h, p, 0].wait_recv()
+            part = view(h, p, (p,))
+            rs[part] = (rs[part].astype(F32) + rb[(0, *part)].astype(F32)).astype(BF)
+            rs_second(h, p)
+
     lanes, subs = iota((PART, 128), 1), iota((PART, 128), 0)
+    sub8 = iota((8, 128), 0)
+    state = {}
 
     def cot_rows(owner, h):
         train_k = 32 * ((subs + h * PART) // 4) + 4 * owner + subs % 4
         total = jnp.zeros((PART, 128), F32)
         for r in range(4):
-            row = jnp.broadcast_to(cots[r:r + 1], (PART, 128))
+            row = jnp.broadcast_to(state["cots"][r:r + 1], (PART, 128))
             total = total + jnp.where(lanes + 128 * r == train_k, row, 0.0)
         return jnp.sum(total, axis=1, keepdims=True)
 
-    sub8 = iota((8, 128), 0)
-    vec = jnp.zeros((1, HALF), F32)
-    score = jnp.zeros((1, 128), F32)
-    for h in range(CHUNKS):
+    def middle(h):
+        if h == 0:
+            state["sum"] = a_last()
+            state["cots"] = state["sum"][8:12]
+            state["head"] = unfold(state["sum"])
+            state["vec"] = jnp.zeros((1, HALF), F32)
+            state["score"] = jnp.zeros((1, 128), F32)
+        unit_head = state["head"]
         cot_here = cot_rows(block, h)
         back = cot_here * unit_head
         summed = []
         for p in range(3):
-            rs_copies[h, p, 2].wait_recv()
-            part = view(h, p, (0, 1, 2))
-            width = CUTS[h][p + 1] - CUTS[h][p]
-            summed.append((rs[part].astype(F32) + rb[(2, *part)].astype(F32)).reshape(PART, width))
+            part = view(h, p, every)
+            total = rs[part].astype(F32)
+            for n in (2, 3, 1):
+                rs_copies[h, p, n].wait_recv()
+                total = total + rb[(n, *part)].astype(F32)
+            summed.append(total.reshape(PART, CUTS[h][p + 1] - CUTS[h][p]))
         summed = jnp.concatenate(summed, axis=1)
         gate, up = summed[:, 0:HALF], summed[:, HALF:2 * HALF]
         sig = jax.nn.sigmoid(gate)
@@ -242,35 +294,30 @@
         lb[(*spot, gates)] = gate_low.reshape(1, 1, 1, PART, HALF)
         lb[(*spot, ups)] = up_low.reshape(1, 1, 1, PART, HALF)
         for p in range(3):
-            ag_start(h, p, 0)
+            ag_first(h, p)
         hidden = (swish * up).astype(BF).astype(F32)
-        vec = vec + jnp.sum(hidden * cot_here, axis=0, keepdims=True)
+        state["vec"] = state["vec"] + jnp.sum(hidden * cot_here, axis=0, keepdims=True)
         score_col = jnp.sum(hidden * unit_head, axis=1, keepdims=True)
         spot = lanes == subs + h * PART + ROWS * (block % 2)
-        score = score + jnp.sum(jnp.where(spot, score_col, 0.0), axis=0, keepdims=True)
-
-    b_send[...] = jnp.zeros_like(b_send)
-    b_send[0, 0:1, :] = vec
-    b_send[0, 8:16, 0:128] = jnp.where(sub8 == block // 2, score, 0.0)
-    b_copies = [remote(b_send.at[0], b_got.at[0], b_s.at[0], b_r.at[0], near[0])]
-    for s in range(2):
-        for h in range(CHUNKS):
-            for p in range(3):
-                ag_copies[h, p, s].wait_recv()
-                ag_start(h, p, s + 1)
-        b_copies[s].wait_recv()
-        b_send[s + 1] = b_send[s] + b_got[s]
-        b_copies.append(remote(b_send.at[s + 1], b_got.at[s + 1], b_s.at[s + 1], b_r.at[s + 1], near[s + 1]))
+        state["score"] = state["score"] + jnp.sum(jnp.where(spot, score_col, 0.0), axis=0, keepdims=True)
+        if h == CHUNKS - 1:
+            b_first(state["vec"], state["score"])
+
+    def spread(h):
+        for p in range(3):
+            for n in (2, 3, 1):
+                ag_copies[h, p, n].wait_recv()
+            ag_second(h, p)
+
     def low(h):
         return lb[h].reshape(8 * PART, 2 * HALF)
 
-    z_copies, t_copies = [], {}
-    for h in range(CHUNKS):
+    def back_products(h):
         for p in range(3):
-            ag_copies[h, p, 2].wait_recv()
+            ag_copies[h, p, 0].wait_recv()
         for c in (0, 256):
             z_send[h, :, c:c + 256] = dot_t(low(h), wb[1, c:c + 256, :]).astype(BF)
-        z_copies.append(remote(z_send.at[h], z_got.at[h], z_s.at[h], z_r.at[h], sib))
+        z_copies[h] = remote(z_send.at[h], z_got.at[h], z_s.at[h], z_r.at[h], sib)
         own = [dot_t(low(h), wb[0, c:c + 256, :]) for c in (0, 256)]
         z_copies[h].wait_recv()
         for n, c in enumerate((0, 256)):
@@ -280,21 +327,23 @@
             t_copies[h, k] = remote(
                 z_own.at[h, xor(j, k, 3)], t_got.at[h, k], t_s.at[8 * h + k], t_r.at[8 * h + k], t_peer[k]
             )
-        if h == 0:
-            b_copies[2].wait_recv()
-            b_send[3] = b_send[2] + b_got[2]
-            b_copies.append(remote(b_send.at[3], b_got.at[3], b_s.at[3], b_r.at[3], sib))
-    b_copies[3].wait_recv()
-    s_send[...] = b_send[3, 8:16, 0:128] + b_got[3, 8:16, 0:128]
+
+    z_copies, t_copies = {}, {}
+    events = sorted((h * SHIFT + e * STEP, h, e) for h in range(CHUNKS) for e in range(5))
+    for _, h, e in events:
+        (products, halve, middle, spread, back_products)[e](h)
+        if h == CHUNKS - 1 and e == 3:
+            b_second()
+    b_copies[7].wait_recv()
+    s_send[...] = b_send[1, 8:16] + b_got[7, 8:16]
     sc_copies = [remote(s_send, s_got.at[k], sc_s.at[k], sc_r.at[k], t_peer[k]) for k in range(1, 8)]
     def grad(v, lo, width):
-        total = jnp.zeros((512, width), F32)
-        for h in range(CHUNKS):
-            lows = lb[h, :, :, :, :, lo:lo + width].reshape(8 * PART, width)
-            total = total + lax.dot_general(
-                x_part(v, h), lows, (((0,), (0,)), ((), ())), preferred_element_type=F32
-            )
-        return total.astype(BF)
+        lows = [lb[h, :, :, :, :, lo:lo + width].reshape(8 * PART, width) for h in range(CHUNKS)]
+        rows = [x_part(v, h) for h in range(CHUNKS)]
+        return lax.dot_general(
+            jnp.concatenate(rows, axis=0), jnp.concatenate(lows, axis=0), (((0,), (0,)), ((), ())),
+            preferred_element_type=F32,
+        ).astype(BF)
 
     for lo in range(0, 2 * HALF, 256):
         g_sib[:, lo:lo + 256] = grad(1, lo, 256)
@@ -314,7 +363,7 @@
     seat = i % each
 
     def d_copy(h, k):
-        there = each * h + xor(seat, k, 3)
+        there = each * h + xor(seat, k, each.bit_length() - 1)
         return pltpu.make_async_remote_copy(
             src_ref=d_send.at[there], dst_ref=rows_out.at[i],
             send_sem=d_s.at[each * h + k], recv_sem=d_r.at[each * (i // each) + k],
@@ -348,21 +397,21 @@
     split = jnp.concatenate([high, middle, last, jnp.zeros((13, 512), BF)], axis=0)
     moved = dot(split, place[...])
     moved = moved[0:1] + moved[1:2] + moved[2:3]
-    score = a_sum[1:2, 0:ROWS]
+    score = state["sum"][7:8, 0:ROWS]
     for b in range(8):
         score = score + jnp.where(j == b, moved[:, b * ROWS:(b + 1) * ROWS], 0.0)
     score_out[...] = jnp.zeros_like(score_out)
     score_out[0:1, 0:ROWS] = score
     head_float = head_row.astype(F32)
-    for v, source in ((core, b_send), (1 - core, b_got)):
+    for v, tile in ((core, b_send[1]), (1 - core, b_got[7])):
         for c in range(0, HALF, 128):
-            column = jnp.broadcast_to(source[3, 0:1, c:c + 128], (128, 128)).T
+            column = jnp.broadcast_to(tile[c // 128:c // 128 + 1], (128, 128)).T
             rows = pl.ds(pl.multiple_of(v * HALF + c, 128), 128)
             down_out[rows, :] = (jnp.concatenate([column] * 4, axis=1) * head_float).astype(BF)
     for half in range(CHUNKS):
         for k in range(each):
             got = pltpu.make_async_remote_copy(
-                src_ref=d_send.at[0], dst_ref=rows_out.at[each * half + xor(seat, k, 3)],
+                src_ref=d_send.at[0], dst_ref=rows_out.at[each * half + xor(seat, k, each.bit_length() - 1)],
                 send_sem=d_s.at[0], recv_sem=d_r.at[each * half + k],
                 device_id=sib, device_id_type=MESH,
             )
@@ -421,14 +470,14 @@
             pltpu.VMEM((2 * HALF, 512), BF),
             pltpu.VMEM((512, 512), BF),
             pltpu.VMEM(cube, BF),
-            pltpu.VMEM((3, *cube), BF),
+            pltpu.VMEM((4, *cube), BF),
             pltpu.VMEM(cube, BF),
             pltpu.VMEM((8, 128), F32),
             pltpu.VMEM((8, 8, 128), F32),
-            pltpu.VMEM((5, 8, HALF), F32),
-            pltpu.VMEM((4, 8, HALF), F32),
-            pltpu.VMEM((4, 16, HALF), F32),
-            pltpu.VMEM((4, 16, HALF), F32),
+            pltpu.VMEM((3, 16, 128), F32),
+            pltpu.VMEM((8, 16, 128), F32),
+            pltpu.VMEM((2, 16, 128), F32),
+            pltpu.VMEM((8, 16, 128), F32),
             pltpu.VMEM((CHUNKS, 8 * PART, 512), BF),
             pltpu.VMEM((CHUNKS, 8 * PART, 512), BF),
             pltpu.VMEM((CHUNKS, 8, PART, 512), BF),
@@ -437,8 +486,8 @@
             pltpu.VMEM((8, 8, 128), F32),
             pltpu.VMEM((512, 2 * HALF), BF),
             pltpu.VMEM((16, 16, 128), BF),
-            *[dma((8,))] * 6, dma((2,)), dma((2,)), dma((7,)), dma((9 * CHUNKS,)), dma((9 * CHUNKS,)),
-            dma((4,)), dma((4,)), dma((9 * CHUNKS,)), dma((9 * CHUNKS,)), dma((4,)), dma((4,)),
+            *[dma((8,))] * 6, dma((2,)), dma((2,)), dma((7,)), dma((12 * CHUNKS,)), dma((12 * CHUNKS,)),
+            dma((8,)), dma((8,)), dma((12 * CHUNKS,)), dma((12 * CHUNKS,)), dma((8,)), dma((8,)),
             dma((CHUNKS,)), dma((CHUNKS,)), dma((8 * CHUNKS,)), dma((8 * CHUNKS,)), dma((8,)), dma((8,)), dma((2,)), dma((2,)), dma((16,)), dma((16,)),
         ],
         compiler_params=pltpu.CompilerParams(

time: 70.4 us -> 68.8 us (0.977)
  Pallas kernels: 69.6 us -> 68 us
    pallas_call x1, Pallas kernels: 66.5 us -> 64.9 us  [per_device(): pl.pallas_call(kernel, name='critic', out_shape=(pltpu.VMEM((512, 2 * HAL...]
where the time goes in v4:
time: 68.8 us; the launch traced here: 68.6 us
  Pallas kernels  68 us (99%)
    pallas_call x1, Pallas kernels, per_device(): pl.pallas_call(kernel, name='critic', out_shape=(pltpu.VMEM((512, 2 * HAL...  64.9 us
    pallas_call x1, Pallas kernels, finish_call(): pl.pallas_call(finish_kernel, name='deliver', out_shape=(jax.ShapeDtypeSt...  3.1 us

profile of v4, /device:TPU:9, one launch (start us, length us, event | category | flops | bytes accessed | tf_op | source)
XLA Modules:
  0.0 68.6 jit_solution(13371479950105139950)
XLA Ops:
  0.6 64.9 %critic.1 = (bf16[512,1792]{1,0:T(8,128)(2,1)S(1)}, bf16[512,1792]{1,0:T(8,128)(2,1)S(1)}, bf16[1792,512]{1,0:T(8,128)(2,1)S(1)}, f32[8,128]{1,0:T(8,128)S(1)}, bf16[16,16,128]{2,1,0:T(8,128)(2,1)S(1)}) custom-call(bf16[64,512]{1,0:T(8,128)(2,1)} %x_hbm.1, s32[512]{0:T(512)} %order_hbm.1, bf16[512]{0:T(512)(128)(2,1)} %head_hbm.1, f32[4]{0:T(128)} %cot_hbm.1, ...), custom_call_target="tpu_custom_call" | custom-call | flops 6000000000 | bytes 12000000 | tf_op jit(solution)/shard_map/critic/pallas_call | solution.py:450
  65.5 3.1 %deliver.1 = (bf16[512,1792]{1,0:T(8,128)(2,1)}, bf16[512,1792]{1,0:T(8,128)(2,1)}, bf16[1792,512]{1,0:T(8,128)(2,1)}, f32[64]{0:T(128)}, bf16[4,8192]{1,0:T(4,128)(2,1)}) custom-call(bf16[512,1792]{1,0:T(8,128)(2,1)S(1)} %get-tuple-element.15.gate_in, bf16[512,1792]{1,0:T(8,128)(2,1)S(1)} %get-tuple-element.16.up_in, ...), custom_call_target="tpu_custom_call" | custom-call | tf_op jit(solution)/shard_map/deliver/pallas_call | solution.py:508

commit v5 on v4

--- a/solution.py
+++ b/solution.py
@@ -11,11 +11,10 @@
 F32 = jnp.float32
 MESH = pl.DeviceIdType.MESH
 HALF = 896
-CHUNKS = 2
-ROWS = 64
-PART = ROWS // CHUNKS
-CHUNKS = 2
-STEP, SHIFT = 3.0, 1.1
+CHUNKS = 4
+STEP = 3.0
+STARTS = (0.0, 0.3, 1.6, 2.6)
+GROUPS = ((0, 2), (2, 1), (3, 1))
 ROWS = 64
 PART = ROWS // CHUNKS
 CUTS = ((0, 640, 1280, 2 * HALF), (0, 512, 1152, 2 * HALF), (0, 640, 1152, 2 * HALF), (0, 640, 1280, 2 * HALF))
@@ -313,23 +312,31 @@
         return lb[h].reshape(8 * PART, 2 * HALF)
 
     def back_products(h):
+        first, count = [g for g in GROUPS if g[0] <= h < g[0] + g[1]][0]
         for p in range(3):
             ag_copies[h, p, 0].wait_recv()
+        if h < first + count - 1:
+            return
+        members = range(first, first + count)
+        group = pl.ds(first, count)
+        lows = jnp.concatenate([low(m) for m in members], axis=0)
         for c in (0, 256):
-            z_send[h, :, c:c + 256] = dot_t(low(h), wb[1, c:c + 256, :]).astype(BF)
-        z_copies[h] = remote(z_send.at[h], z_got.at[h], z_s.at[h], z_r.at[h], sib)
-        own = [dot_t(low(h), wb[0, c:c + 256, :]) for c in (0, 256)]
-        z_copies[h].wait_recv()
+            part = dot_t(lows, wb[1, c:c + 256, :]).astype(BF)
+            z_send[first:first + count, :, c:c + 256] = part.reshape(count, 8 * PART, 256)
+        copy = remote(z_send.at[group], z_got.at[group], z_s.at[first], z_r.at[first], sib)
+        own = [dot_t(lows, wb[0, c:c + 256, :]) for c in (0, 256)]
+        copy.wait_recv()
         for n, c in enumerate((0, 256)):
-            both = own[n] + z_got[h, :, c:c + 256].astype(F32)
-            z_own[h, :, :, c:c + 256] = both.astype(BF).reshape(8, PART, 256)
+            both = own[n].reshape(count, 8 * PART, 256) + z_got[first:first + count, :, c:c + 256].astype(F32)
+            z_own[first:first + count, :, :, c:c + 256] = both.astype(BF).reshape(count, 8, PART, 256)
         for k in far:
-            t_copies[h, k] = remote(
-                z_own.at[h, xor(j, k, 3)], t_got.at[h, k], t_s.at[8 * h + k], t_r.at[8 * h + k], t_peer[k]
+            t_copies[first, k] = remote(
+                z_own.at[group, xor(j, k, 3)], t_got.at[group, k],
+                t_s.at[8 * first + k], t_r.at[8 * first + k], t_peer[k],
             )
 
-    z_copies, t_copies = {}, {}
-    events = sorted((h * SHIFT + e * STEP, h, e) for h in range(CHUNKS) for e in range(5))
+    t_copies = {}
+    events = sorted((STARTS[h] + e * STEP, h, e) for h in range(CHUNKS) for e in range(5))
     for _, h, e in events:
         (products, halve, middle, spread, back_products)[e](h)
         if h == CHUNKS - 1 and e == 3:
@@ -373,7 +380,8 @@
     for h in range(CHUNKS):
         total = z_own[h, pl.ds(j, 1)].reshape(PART, 512).astype(F32)
         for k in far:
-            t_copies[h, k].wait_recv()
+            if (h, k) in t_copies:
+                t_copies[h, k].wait_recv()
             total = total + t_got[h, k].astype(F32)
         low_rows = (total + cot_rows(j, h) * head_row.astype(F32)).astype(BF)
         stacked = jnp.concatenate([low_rows[:, c:c + 128] for c in range(0, 512, 128)], axis=0)

time: 68.8 us -> 66.8 us (0.971)
  Pallas kernels: 68 us -> 65.8 us
    pallas_call x1, Pallas kernels: 64.9 us -> 62.7 us  [per_device(): pl.pallas_call(kernel, name='critic', out_shape=(pltpu.VMEM((512, 2 * HAL...]
where the time goes in v5:
time: 66.8 us; the launch traced here: 66.4 us
  Pallas kernels  65.8 us (99%)
    pallas_call x1, Pallas kernels, per_device(): pl.pallas_call(kernel, name='critic', out_shape=(pltpu.VMEM((512, 2 * HAL...  62.7 us
    pallas_call x1, Pallas kernels, finish_call(): pl.pallas_call(finish_kernel, name='deliver', out_shape=(jax.ShapeDtypeSt...  3.1 us

profile of v5, /device:TPU:9, one launch (start us, length us, event | category | flops | bytes accessed | tf_op | source)
XLA Modules:
  0.0 66.4 jit_solution(1750359901486727287)
XLA Ops:
  0.6 62.7 %critic.1 = (bf16[512,1792]{1,0:T(8,128)(2,1)S(1)}, bf16[512,1792]{1,0:T(8,128)(2,1)S(1)}, bf16[1792,512]{1,0:T(8,128)(2,1)S(1)}, f32[8,128]{1,0:T(8,128)S(1)}, bf16[16,16,128]{2,1,0:T(8,128)(2,1)S(1)}) custom-call(bf16[64,512]{1,0:T(8,128)(2,1)} %x_hbm.1, s32[512]{0:T(512)} %order_hbm.1, bf16[512]{0:T(512)(128)(2,1)} %head_hbm.1, f32[4]{0:T(128)} %cot_hbm.1, ...), custom_call_target="tpu_custom_call" | custom-call | flops 6000000000 | bytes 12000000 | tf_op jit(solution)/shard_map/critic/pallas_call | solution.py:458
  63.3 3.1 %deliver.1 = (bf16[512,1792]{1,0:T(8,128)(2,1)}, bf16[512,1792]{1,0:T(8,128)(2,1)}, bf16[1792,512]{1,0:T(8,128)(2,1)}, f32[64]{0:T(128)}, bf16[4,8192]{1,0:T(4,128)(2,1)}) custom-call(bf16[512,1792]{1,0:T(8,128)(2,1)S(1)} %get-tuple-element.15.gate_in, bf16[512,1792]{1,0:T(8,128)(2,1)S(1)} %get-tuple-element.16.up_in, ...), custom_call_target="tpu_custom_call" | custom-call | tf_op jit(solution)/shard_map/deliver/pallas_call | solution.py:516

commit v6 on v5

--- a/solution.py
+++ b/solution.py
@@ -14,7 +14,7 @@
 CHUNKS = 4
 STEP = 3.0
 STARTS = (0.0, 0.3, 1.6, 2.6)
-GROUPS = ((0, 2), (2, 1), (3, 1))
+GROUPS = ((0, 1), (1, 1), (2, 1), (3, 1))
 ROWS = 64
 PART = ROWS // CHUNKS
 CUTS = ((0, 640, 1280, 2 * HALF), (0, 512, 1152, 2 * HALF), (0, 640, 1152, 2 * HALF), (0, 640, 1280, 2 * HALF))
@@ -358,11 +358,6 @@
         remote(g_sib.at[:, gates], gate_out.at[:, mine], g_s.at[0], g_r.at[0], sib),
         remote(g_sib.at[:, ups], up_out.at[:, mine], g_s.at[1], g_r.at[1], sib),
     ]
-    for first, out in ((0, gate_out), (HALF, up_out)):
-        for lo, width in ((0, 256), (256, 256), (512, 256), (768, 128)):
-            where = pl.ds(pl.multiple_of(core * HALF + lo, 128), width)
-            out[:, where] = grad(0, first + lo, width)
-
     want, have = iota((4 * PART, 4 * PART), 0), iota((4 * PART, 4 * PART), 1)
     source = ((want // 4) % 4) * PART + (want // 16) * 4 + want % 4
     gather = (have == source).astype(BF)
@@ -392,6 +387,11 @@
             else:
                 pl.when(i // each != h)(d_copy(h, 0).start)
     rows_out[pl.ds(i, 1)] = d_send[pl.ds(i, 1)]
+
+    for first, out in ((0, gate_out), (HALF, up_out)):
+        for lo, width in ((0, 256), (256, 256), (512, 256), (768, 128)):
+            where = pl.ds(pl.multiple_of(core * HALF + lo, 128), width)
+            out[:, where] = grad(0, first + lo, width)
 
     score = s_send[...]
     for k in range(1, 8):

time: 66.8 us -> 66.3 us (level)
  Pallas kernels: 65.8 us -> 64.8 us
    pallas_call x1, Pallas kernels: 62.7 us -> 61.7 us  [per_device(): pl.pallas_call(kernel, name='critic', out_shape=(pltpu.VMEM((512, 2 * HAL...]
where the time goes in v6:
time: 66.3 us; the launch traced here: 65.5 us
  Pallas kernels  64.8 us (98%)
    pallas_call x1, Pallas kernels, per_device(): pl.pallas_call(kernel, name='critic', out_shape=(pltpu.VMEM((512, 2 * HAL...  61.7 us
    pallas_call x1, Pallas kernels, finish_call(): pl.pallas_call(finish_kernel, name='deliver', out_shape=(jax.ShapeDtypeSt...  3.1 us

profile of v6, /device:TPU:9, one launch (start us, length us, event | category | flops | bytes accessed | tf_op | source)
XLA Modules:
  0.0 65.5 jit_solution(9255219131349378261)
XLA Ops:
  0.6 61.7 %critic.1 = (bf16[512,1792]{1,0:T(8,128)(2,1)S(1)}, bf16[512,1792]{1,0:T(8,128)(2,1)S(1)}, bf16[1792,512]{1,0:T(8,128)(2,1)S(1)}, f32[8,128]{1,0:T(8,128)S(1)}, bf16[16,16,128]{2,1,0:T(8,128)(2,1)S(1)}) custom-call(bf16[64,512]{1,0:T(8,128)(2,1)} %x_hbm.1, s32[512]{0:T(512)} %order_hbm.1, bf16[512]{0:T(512)(128)(2,1)} %head_hbm.1, f32[4]{0:T(128)} %cot_hbm.1, ...), custom_call_target="tpu_custom_call" | custom-call | flops 6000000000 | bytes 12000000 | tf_op jit(solution)/shard_map/critic/pallas_call | solution.py:458
  62.4 3.1 %deliver.1 = (bf16[512,1792]{1,0:T(8,128)(2,1)}, bf16[512,1792]{1,0:T(8,128)(2,1)}, bf16[1792,512]{1,0:T(8,128)(2,1)}, f32[64]{0:T(128)}, bf16[4,8192]{1,0:T(4,128)(2,1)}) custom-call(bf16[512,1792]{1,0:T(8,128)(2,1)S(1)} %get-tuple-element.15.gate_in, bf16[512,1792]{1,0:T(8,128)(2,1)S(1)} %get-tuple-element.16.up_in, ...), custom_call_target="tpu_custom_call" | custom-call | tf_op jit(solution)/shard_map/deliver/pallas_call | solution.py:516
